TPU v7x, 512 devices: a whole 4x4x16 slice. The times are simulated.
512 devices in a mesh: ctx: 32 (over z_hi, x, core), dp: 16 (over z_lo, y).
Axes of the slice: x: 4, y: 4, z: 16 (z_hi: 4, z_lo: 4; z = z_hi * 4 + z_lo), core: 2. Of those that a mesh axis runs over, the one named last changes fastest.
Arguments:
- queries: bfloat16 [16, 4096, 4096], P('dp', 'ctx'), may hold values from -4.5 to 4.5
- key_heads: bfloat16 [16, 4096, 512], P('dp', 'ctx'), may hold values from -4.5 to 4.5
- value_heads: bfloat16 [16, 4096, 512], P('dp', 'ctx'), may hold values from -6 to 6
- out_grad: bfloat16 [16, 4096, 4096], P('dp', 'ctx'), may hold values from -6 to 6
- block_order: int32 [64], replicated, may hold values from 0 to 63, each once
Outputs:
- attn_out: bfloat16 [16, 4096, 4096], P('dp', 'ctx')
- dqueries: bfloat16 [16, 4096, 4096], P('dp', 'ctx')
- dkey_heads: bfloat16 [16, 4096, 512], P('dp', 'ctx')
- dvalue_heads: bfloat16 [16, 4096, 512], P('dp', 'ctx')
- out_factor: float32 [4096, 128], P(('ctx', 'dp'))
- grad_factor: float32 [1024, 256], P(('ctx', 'dp'))
Inputs may be any that keep to these rules, and one draw needn't show every extreme that they name: Slot b lies on ctx index b // 2 (the first 64 tokens for even b, the last 64 for odd b) and holds positions block_order[b] * 64 to block_order[b] * 64 + 63 of every sequence; each value appears once.
All inputs are finite; a program needn't handle non-finite values.
Results may differ from a plain program's by a relative error of at most 0.025.
Values may be sent and summed in bfloat16 or wider, within the bound.
A program may use at most 128 MiB of HBM per device.

v0:
```python
import math

import jax
import jax.numpy as jnp
from jax import lax
from jax.sharding import PartitionSpec as P

HD = 128
STEPS = 4


def from_behind(value, axis, by):
    size = lax.axis_size(axis)
    return lax.ppermute(value, axis, [(i, (i + by) % size) for i in range(size)])


def local(queries, key_heads, value_heads, out_grad, block_order):
    row_count = queries.shape[1]
    half_rows = row_count // 2
    head_count = queries.shape[2] // HD
    kv_count = key_heads.shape[2] // HD
    group_size = head_count // kv_count
    ctx_count = lax.axis_size("ctx")
    my_index = lax.axis_index("ctx")
    scaling = jnp.float32(1.0 / math.sqrt(HD))
    offsets = jnp.arange(half_rows, dtype=jnp.int32)
    stat_shape = (kv_count, group_size, row_count)

    def place_of(device):
        halves = lax.dynamic_slice(block_order, (2 * device,), (2,))
        return (halves[:, None] * half_rows + offsets[None, :]).reshape(row_count)

    own_places = place_of(my_index)
    query_local = queries[0].reshape(row_count, kv_count, group_size, HD)
    grad_local = out_grad[0].reshape(row_count, kv_count, group_size, HD)
    key_now = key_heads[0].reshape(row_count, kv_count, HD)
    value_now = value_heads[0].reshape(row_count, kv_count, HD)

    def visible_scores(key_block, key_places):
        visible = key_places[None, :] <= own_places[:, None]
        scores = (
            jnp.einsum("tgjd,ugd->gjtu", query_local, key_block, preferred_element_type=jnp.float32)
            * scaling
        )
        return (visible[None, None], scores)

    block_stats = []
    kept_blocks = []
    for visit_index in range(STEPS):
        key_places = place_of((my_index - visit_index) % ctx_count)
        forward_visible, forward_scores = visible_scores(key_now, key_places)
        block_max = jnp.max(jnp.where(forward_visible, forward_scores, -jnp.inf), axis=-1)
        has_key = jnp.any(forward_visible, axis=-1)
        safe_max = jnp.where(has_key, block_max, 0.0)
        block_weights = jnp.where(
            forward_visible, jnp.exp(forward_scores - safe_max[..., None]), 0.0
        ).astype(jnp.bfloat16)
        weight_total = jnp.sum(lax.optimization_barrier(block_weights).astype(jnp.float32), axis=-1)
        weighted = jnp.einsum(
            "gjtu,ugd->gjtd", block_weights, value_now, preferred_element_type=jnp.float32
        )
        block_stats.append((jnp.where(has_key, block_max, -jnp.inf), weight_total, weighted))
        kept_blocks.append((key_now, value_now, key_places))
        if visit_index + 1 < STEPS:
            key_now, value_now = from_behind((key_now, value_now), "ctx", 1)
    upper_max = block_stats[0][0]
    for block_entry in block_stats[1:]:
        upper_max = jnp.maximum(upper_max, block_entry[0])
    norm_total = jnp.zeros(stat_shape, jnp.float32)
    mixed_sum = jnp.zeros(stat_shape + (HD,), jnp.float32)
    for block_entry in block_stats:
        factor = jnp.exp(block_entry[0] - upper_max)
        norm_total = norm_total + factor * block_entry[1]
        mixed_sum = mixed_sum + factor[..., None] * block_entry[2]
    attn_rows = jnp.transpose(mixed_sum / norm_total[..., None], (2, 0, 1, 3)).astype(jnp.bfloat16)
    log_total = upper_max + jnp.log(norm_total)
    delta_rows = jnp.transpose(
        jnp.sum(grad_local.astype(jnp.float32) * attn_rows.astype(jnp.float32), axis=-1), (1, 2, 0)
    )
    dquery_sum = jnp.zeros((row_count, kv_count, group_size, HD), jnp.float32)
    for visit_index in range(STEPS):
        key_block, value_block, key_places = kept_blocks[visit_index]
        backward_visible, backward_scores = visible_scores(key_block, key_places)
        prob_full = jnp.where(
            backward_visible, jnp.exp(backward_scores - log_total[..., None]), 0.0
        )
        prob_round = prob_full.astype(jnp.bfloat16)
        dvalue_part = jnp.einsum(
            "gjtu,tgjd->ugd", prob_round, grad_local, preferred_element_type=jnp.float32
        )
        dprob_full = jnp.einsum(
            "tgjd,ugd->gjtu", grad_local, value_block, preferred_element_type=jnp.float32
        )
        dscore = (prob_full * (dprob_full - delta_rows[..., None])).astype(jnp.bfloat16)
        dquery_part = jnp.einsum(
            "gjtu,ugd->tgjd", dscore, key_block, preferred_element_type=jnp.float32
        )
        dkey_part = jnp.einsum(
            "gjtu,tgjd->ugd", dscore, query_local, preferred_element_type=jnp.float32
        )
        dquery_part, dkey_part, dvalue_part = (dquery_part, dkey_part, dvalue_part)
        dquery_sum = dquery_sum + dquery_part
        if visit_index == 0:
            travel = (dkey_part, dvalue_part)
        else:
            moved_back = from_behind((travel[0], travel[1]), "ctx", 1)
            travel = (moved_back[0] + dkey_part, moved_back[1] + dvalue_part)
    home_sum = from_behind((travel[0], travel[1]), "ctx", 1 - STEPS)
    dqueries = (dquery_sum * scaling).astype(jnp.bfloat16).reshape(1, row_count, head_count * HD)
    dkey_round = (home_sum[0] * scaling).astype(jnp.bfloat16)
    dvalue_round = home_sum[1].astype(jnp.bfloat16)
    out_rows = attn_rows.reshape(row_count, head_count, HD)
    joined = jnp.concatenate([dkey_round, dvalue_round], axis=2)
    grad_local_sum = jnp.einsum(
        "tgd,tge->gde", joined, joined, preferred_element_type=jnp.float32
    ).reshape(kv_count * 2 * HD, 2 * HD)
    token_total = row_count * ctx_count * lax.axis_size("dp")
    out_local = jnp.einsum(
        "thd,the->hde", out_rows, out_rows, preferred_element_type=jnp.float32
    ).reshape(head_count * HD, HD)
    out_factor, grad_factor = (
        lax.psum_scatter(out_local, ("ctx", "dp"), scatter_dimension=0, tiled=True),
        lax.psum_scatter(grad_local_sum, ("ctx", "dp"), scatter_dimension=0, tiled=True),
    )
    attn_out = attn_rows.reshape(1, row_count, head_count * HD)
    dkey_heads = dkey_round.reshape(1, row_count, kv_count * HD)
    dvalue_heads = dvalue_round.reshape(1, row_count, kv_count * HD)
    return (
        attn_out,
        dqueries,
        dkey_heads,
        dvalue_heads,
        out_factor / token_total,
        grad_factor / token_total,
    )


def solution(mesh):
    in_specs = (
        P("dp", "ctx", None),
        P("dp", "ctx", None),
        P("dp", "ctx", None),
        P("dp", "ctx", None),
        P(),
    )
    out_specs = (
        P("dp", "ctx", None),
        P("dp", "ctx", None),
        P("dp", "ctx", None),
        P("dp", "ctx", None),
        P(("ctx", "dp"), None),
        P(("ctx", "dp"), None),
    )
    return jax.shard_map(local, mesh=mesh, in_specs=in_specs, out_specs=out_specs, check_vma=False)
```

profile of v0, /device:TPU:1, one launch (start us, length us, event | category | flops | bytes accessed | tf_op | source)
XLA Modules:
  0.0 655.3 jit_solution(14282415667039716327)
XLA Ops:
  7.2 1.0 copy.137
  8.2 0.8 copy.140
  9.0 4.5 collective-permute-start
  13.5 1.0 copy.144
  14.5 1.9 collective-permute-start.3
  16.6 0.9 dynamic-slice_multiply_fusion.6
  18.1 0.8 compare_reduce_fusion
  18.9 0.7 broadcast_compare_fusion
  19.6 1.5 copy.239
  21.1 0.7 fusion.31
  21.8 1.3 copy-done
  23.5 1.6 copy.149
  25.9 0.7 fusion.25
  26.6 0.5 fusion.28
  27.1 3.5 collective-permute-start.1
  30.6 1.3 fusion.85
  31.9 1.9 collective-permute-start.4
  34.1 0.7 fusion.19
  35.3 3.2 collective-permute-start.2
  38.9 1.9 collective-permute-start.5
  41.0 6.5 collective-permute-done.2
  47.6 0.7 fusion.13
  49.0 0.9 copy-done.1
  49.9 0.5 convolution_bitcast_fusion.3
  50.4 2.6 collective-permute-start.10
  53.1 1.1 multiply_reduce_fusion
  54.2 0.8 fusion.7
  55.0 0.6 convolution_bitcast_fusion.7
  55.9 2.1 collective-permute-start.6
  58.0 1.7 fusion.5
  59.7 0.8 fusion.3
  60.5 0.8 fusion.1
  61.3 2.2 fusion.115
  63.4 0.6 convolution_bitcast_fusion.5
  64.0 6.1 collective-permute-done.6
  70.2 0.6 fusion.41
  70.8 1.9 collective-permute-start.7
  72.7 0.5 fusion.42
  73.3 1.9 collective-permute-start.11
  75.2 26.3 %collective-permute-done.7 = f32[128,4,128]{2,0,1:T(8,128)S(1)} collective-permute-done((f32[128,4,128]{2,0,1:T(8,128)S(1)}, f32[128,4,128]{2,0,1:T(8,128)S(1)}, u32[]{:S(2)}, u32[]{:S(2)}) %collective-permute-start.7) | collective-permute-done | bytes 262176 | tf_op jit(solution)/shard_map/ppermute | solution.py:14
  101.5 1.9 collective-permute-start.8
  103.5 0.5 convolution_bitcast_fusion.1
  104.0 0.6 convolution_bitcast_fusion.4
  104.7 1.9 collective-permute-start.12
  106.6 18.2 %collective-permute-done.8 = f32[128,4,128]{2,0,1:T(8,128)S(1)} collective-permute-done((f32[128,4,128]{2,0,1:T(8,128)S(1)}, f32[128,4,128]{2,0,1:T(8,128)S(1)}, u32[]{:S(2)}, u32[]{:S(2)}) %collective-permute-start.8) | collective-permute-done | bytes 262176 | tf_op jit(solution)/shard_map/ppermute | solution.py:14
  124.8 11.8 %collective-permute-start.9 = (f32[128,4,128]{2,0,1:T(8,128)S(1)}, f32[128,4,128]{2,0,1:T(8,128)S(1)}, u32[]{:S(2)}, u32[]{:S(2)}) collective-permute-start(f32[128,4,128]{2,0,1:T(8,128)S(1)} %add.267), channel_id=1, source_target_pairs={{0,464},{16,480},{32,496},{48,0},{64,16},{80,32},{96,48},{112,64},... | collective-permute-start | bytes 786440 | tf_op jit(solution)/shard_map/ppermute | solution.py:14
  136.6 0.5 convolution_bitcast_fusion
  137.1 1.9 collective-permute-start.13
  139.1 0.9 collective-permute-done.9
  140.1 5.2 collective-permute-done.13
  145.3 1.4 fusion.63
  147.1 0.8 copy-done.3
  147.9 0.5 fusion.92
  148.4 0.7 copy-done.7
  149.1 0.5 fusion.89
  149.6 0.7 copy-done.9
  150.4 0.6 multiply_convert_fusion
  151.0 1.3 copy.178
  152.3 1.3 copy.177
  153.8 0.8 copy.180
  154.7 0.8 copy.179
  155.5 490.4 %all-reduce.5.cloned.1.call-done = (f32[4096,128]{1,0:T(8,128)}, f32[1024,256]{1,0:T(8,128)}) async-done(((f32[4096,128]{1,0:T(8,128)}, f32[1024,256]{1,0:T(8,128)}), (f32[4096,128]{1,0:T(8,128)}, f32[1024,256]{1,0:T(8,128)})) %all-reduce.5.cloned.1.call-update) | async-done | bytes 3145744
  645.9 1.3 dynamic-slice_multiply_fusion
  647.2 1.3 dynamic-slice_multiply_fusion.1
  (90 shorter events, 5.2 us)
Async XLA Ops:
  7.2 638.7 %all-reduce.5.cloned.1.call-start = ((), (), s32[]{:S(2)}) async-start(), calls=%async_computation | async-start | bytes 6291456
  9.0 16.8 %collective-permute-start = (bf16[128,4,128]{2,0,1:T(8,128)(2,1)}, bf16[128,4,128]{2,0,1:T(8,128)(2,1)S(1)}, u32[]{:S(2)}, u32[]{:S(2)}) collective-permute-start(bf16[128,4,128]{2,0,1:T(8,128)(2,1)} %copy.140), channel_id=1, source_target_pairs={{0,16},{16,32},{32,48},{48,64},{64,80},{80,96},{96,112},{112,128},... | collective-permute-start | bytes 393224 | tf_op jit(solution)/shard_map/ppermute | solution.py:14
  14.5 16.0 %collective-permute-start.3 = (bf16[128,4,128]{0,2,1:T(8,128)(2,1)S(1)}, bf16[128,4,128]{0,2,1:T(8,128)(2,1)}, u32[]{:S(2)}, u32[]{:S(2)}) collective-permute-start(bf16[128,4,128]{0,2,1:T(8,128)(2,1)S(1)} %bitcast.374), channel_id=1, source_target_pairs={{0,16},{16,32},{32,48},{48,64},{64,80},{80,96},{96,112},{112,128},... | collective-permute-start | bytes 393224 | tf_op jit(solution)/shard_map/ppermute | solution.py:14
  18.9 2.9 copy-start.25
  19.6 2.2 copy-start.18
  21.7 1.3 copy-start
  21.7 1.3 copy-start.20
  25.2 0.7 copy-start.17
  25.6 0.9 copy-start.23
  25.8 1.2 copy-start.10
  27.1 7.0 %copy-start.16 = (pred[128,128]{0,1:T(8,128)(4,1)S(1)}, pred[128,128]{0,1:T(8,128)(4,1)}, u32[]{:S(2)}) copy-start(pred[128,128]{0,1:T(8,128)(4,1)} %get-tuple-element.43) | copy-start | bytes 49156
  27.1 7.0 %collective-permute-start.1 = (bf16[128,4,128]{2,0,1:T(8,128)(2,1)S(1)}, bf16[128,4,128]{2,0,1:T(8,128)(2,1)S(1)}, u32[]{:S(2)}, u32[]{:S(2)}) collective-permute-start(bf16[128,4,128]{2,0,1:T(8,128)(2,1)S(1)} %collective-permute-done), channel_id=1, source_target_pairs={{0,16},{16,32},{32,48},{48,64},{64,80},{80,96},{96,112},{112,128},... | collective-permute-start | bytes 393224 | tf_op jit(solution)/shard_map/ppermute | solution.py:14
  31.9 2.9 copy-start.24
  31.9 6.6 %collective-permute-start.4 = (bf16[128,4,128]{0,2,1:T(8,128)(2,1)}, bf16[128,4,128]{0,2,1:T(8,128)(2,1)S(1)}, u32[]{:S(2)}, u32[]{:S(2)}) collective-permute-start(bf16[128,4,128]{0,2,1:T(8,128)(2,1)} %collective-permute-done.3), channel_id=1, source_target_pairs={{0,16},{16,32},{32,48},{48,64},{64,80},{80,96},{96,112},{112,128},... | collective-permute-start | bytes 393224 | tf_op jit(solution)/shard_map/ppermute | solution.py:14
  34.1 1.2 copy-start.12
  35.3 12.3 %collective-permute-start.2 = (bf16[128,4,128]{2,0,1:T(8,128)(2,1)S(1)}, bf16[128,4,128]{2,0,1:T(8,128)(2,1)S(1)}, u32[]{:S(2)}, u32[]{:S(2)}) collective-permute-start(bf16[128,4,128]{2,0,1:T(8,128)(2,1)S(1)} %collective-permute-done.1), channel_id=1, source_target_pairs={{0,16},{16,32},{32,48},{48,64},{64,80},{80,96},{96,112},{112,128},... | collective-permute-start | bytes 393224 | tf_op jit(solution)/shard_map/ppermute | solution.py:14
  38.9 9.3 %copy-start.22 = (pred[128]{0:T(512)(128)(4,1)S(1)}, pred[128]{0:T(512)(128)(4,1)}, u32[]{:S(2)}) copy-start(pred[128]{0:T(512)(128)(4,1)} %get-tuple-element.30) | copy-start | bytes 388
  38.9 14.1 %collective-permute-start.5 = (bf16[128,4,128]{0,2,1:T(8,128)(2,1)S(1)}, bf16[128,4,128]{0,2,1:T(8,128)(2,1)S(1)}, u32[]{:S(2)}, u32[]{:S(2)}) collective-permute-start(bf16[128,4,128]{0,2,1:T(8,128)(2,1)S(1)} %collective-permute-done.4), channel_id=1, source_target_pairs={{0,16},{16,32},{32,48},{48,64},{64,80},{80,96},{96,112},{112,128},... | collective-permute-start | bytes 393224 | tf_op jit(solution)/shard_map/ppermute | solution.py:14
  48.3 0.7 copy-start.21
  48.3 0.7 copy-start.26
  48.3 1.6 copy-start.1
  48.3 1.6 copy-start.19
  50.4 22.3 %collective-permute-start.10 = (f32[128,4,128]{2,0,1:T(8,128)S(1)}, f32[128,4,128]{2,0,1:T(8,128)S(1)}, u32[]{:S(2)}, u32[]{:S(2)}) collective-permute-start(f32[128,4,128]{2,0,1:T(8,128)S(1)} %convolution_bitcast_fusion.3), channel_id=1, source_target_pairs={{0,16},{16,32},{32,48},{48,64},{64,80},{80,96},{96,112},{112,128},... | collective-permute-start | bytes 786440 | tf_op jit(solution)/shard_map/ppermute | solution.py:14
  54.9 1.0 copy-start.4
  55.9 14.3 %collective-permute-start.6 = (f32[128,4,128]{2,0,1:T(8,128)S(1)}, f32[128,4,128]{2,0,1:T(8,128)S(1)}, u32[]{:S(2)}, u32[]{:S(2)}) collective-permute-start(f32[128,4,128]{2,0,1:T(8,128)S(1)} %convolution_bitcast_fusion.7), channel_id=1, source_target_pairs={{0,16},{16,32},{32,48},{48,64},{64,80},{80,96},{96,112},{112,128},... | collective-permute-start | bytes 786440 | tf_op jit(solution)/shard_map/ppermute | solution.py:14
  59.7 10.5 %copy-start.2 = (bf16[4,8,128,128]{2,3,1,0:T(8,128)(2,1)}, bf16[4,8,128,128]{2,3,1,0:T(8,128)(2,1)S(1)}, u32[]{:S(2)}) copy-start(bf16[4,8,128,128]{2,3,1,0:T(8,128)(2,1)S(1)} %fusion.5) | copy-start | bytes 3145732
  60.5 3.0 copy-start.6
  61.2 42.7 %copy-start.8 = (bf16[4,8,128,128]{2,3,1,0:T(8,128)(2,1)}, bf16[4,8,128,128]{2,3,1,0:T(8,128)(2,1)S(1)}, u32[]{:S(2)}) copy-start(bf16[4,8,128,128]{2,3,1,0:T(8,128)(2,1)S(1)} %fusion.1) | copy-start | bytes 3145732
  70.8 30.7 %collective-permute-start.7 = (f32[128,4,128]{2,0,1:T(8,128)S(1)}, f32[128,4,128]{2,0,1:T(8,128)S(1)}, u32[]{:S(2)}, u32[]{:S(2)}) collective-permute-start(f32[128,4,128]{2,0,1:T(8,128)S(1)} %fusion.41), channel_id=1, source_target_pairs={{0,16},{16,32},{32,48},{48,64},{64,80},{80,96},{96,112},{112,128},... | collective-permute-start | bytes 786440 | tf_op jit(solution)/shard_map/ppermute | solution.py:14
  73.3 31.3 %collective-permute-start.11 = (f32[128,4,128]{2,0,1:T(8,128)S(1)}, f32[128,4,128]{2,0,1:T(8,128)S(1)}, u32[]{:S(2)}, u32[]{:S(2)}) collective-permute-start(f32[128,4,128]{2,0,1:T(8,128)S(1)} %fusion.42), channel_id=1, source_target_pairs={{0,16},{16,32},{32,48},{48,64},{64,80},{80,96},{96,112},{112,128},... | collective-permute-start | bytes 786440 | tf_op jit(solution)/shard_map/ppermute | solution.py:14
  101.5 23.2 %collective-permute-start.8 = (f32[128,4,128]{2,0,1:T(8,128)S(1)}, f32[128,4,128]{2,0,1:T(8,128)S(1)}, u32[]{:S(2)}, u32[]{:S(2)}) collective-permute-start(f32[128,4,128]{2,0,1:T(8,128)S(1)} %add.266), channel_id=1, source_target_pairs={{0,16},{16,32},{32,48},{48,64},{64,80},{80,96},{96,112},{112,128},... | collective-permute-start | bytes 786440 | tf_op jit(solution)/shard_map/ppermute | solution.py:14
  104.7 32.5 %collective-permute-start.12 = (f32[128,4,128]{2,0,1:T(8,128)S(1)}, f32[128,4,128]{2,0,1:T(8,128)S(1)}, u32[]{:S(2)}, u32[]{:S(2)}) collective-permute-start(f32[128,4,128]{2,0,1:T(8,128)S(1)} %add.269), channel_id=1, source_target_pairs={{0,16},{16,32},{32,48},{48,64},{64,80},{80,96},{96,112},{112,128},... | collective-permute-start | bytes 786440 | tf_op jit(solution)/shard_map/ppermute | solution.py:14
  124.8 15.2 %collective-permute-start.9 = (f32[128,4,128]{2,0,1:T(8,128)S(1)}, f32[128,4,128]{2,0,1:T(8,128)S(1)}, u32[]{:S(2)}, u32[]{:S(2)}) collective-permute-start(f32[128,4,128]{2,0,1:T(8,128)S(1)} %add.267), channel_id=1, source_target_pairs={{0,464},{16,480},{32,496},{48,0},{64,16},{80,32},{96,48},{112,64},... | collective-permute-start | bytes 786440 | tf_op jit(solution)/shard_map/ppermute | solution.py:14
  137.1 8.2 %collective-permute-start.13 = (bf16[128,4,128]{2,0,1:T(8,128)(2,1)S(1)}, bf16[128,4,128]{2,0,1:T(8,128)(2,1)S(1)}, u32[]{:S(2)}, u32[]{:S(2)}) collective-permute-start(bf16[128,4,128]{2,0,1:T(8,128)(2,1)S(1)} %add.270), channel_id=1, source_target_pairs={{0,464},{16,480},{32,496},{48,0},{64,16},{80,32},{96,48},{112,64},... | collective-permute-start | bytes 393224 | tf_op jit(solution)/shard_map/ppermute | solution.py:14
  140.0 6.7 %copy-start.5 = (bf16[4,8,128,128]{2,3,1,0:T(8,128)(2,1)S(1)}, bf16[4,8,128,128]{2,3,1,0:T(8,128)(2,1)}, u32[]{:S(2)}) copy-start(bf16[4,8,128,128]{2,3,1,0:T(8,128)(2,1)} %copy-done.4) | copy-start | bytes 3145732
  145.3 1.4 copy-start.14
  146.7 1.2 copy-start.3
  146.7 1.2 copy-start.11
  147.9 1.2 copy-start.7
  147.9 1.2 copy-start.13
  149.1 1.2 copy-start.9
  151.0 2.6 copy-start.15
Sparse Core Ops, SparseCore 0:
  146.8 499.0 all-reduce.4
where the time goes:
time: 657 us; the launch traced here: 655 us
  waiting for transfers between devices  554 us (84%)
  starting transfers between devices  43 us (7%)
  matrix products  19.9 us (3%)
  local copies, waits for them, and re-layouts  15.6 us (2%)
  between operations  14.8 us (2%)
  other arithmetic  8.05 us (1%)
    unnamed x2, waiting for transfers between devices  490 us
    ppermute x14, waiting for transfers between devices, from_behind(): lax.ppermute(value, axis, [(i, (i + by) % size) for i in range(size)])  63.4 us
    ppermute x14, starting transfers between devices, from_behind(): lax.ppermute(value, axis, [(i, (i + by) % size) for i in range(size)])  43 us
    unnamed x62, local copies, waits for them, and re-layouts  14.2 us
  transfers between devices with their start and end apart: 15, of which 8 were waited for; matrix products, arithmetic and copies ran while one was open for 5% of the time, Pallas kernels for 0%

commit v1 on v0

v1 whole, which is shorter than its diff:
```python
import math

import jax
import jax.numpy as jnp
from jax import lax
from jax.experimental import pallas as pl
from jax.experimental.pallas import tpu as pltpu
from jax.sharding import PartitionSpec as P

HD = 128
STEPS = 4
TOK = 128
KVH = 4
NEG = -1e30
LOG2E = 1.0 / math.log(2.0)
SCALE = 1.0 / math.sqrt(HD)
MESH = pl.DeviceIdType.MESH
BF = jnp.bfloat16
F32 = jnp.float32


def dot(a, b, ca, cb):
    return lax.dot_general(a, b, (((ca,), (cb,)), ((), ())), preferred_element_type=F32)


class Place:
    def __init__(self):
        c, d = lax.axis_index("ctx"), lax.axis_index("dp")
        self.zh, self.x, self.core = c // 8, (c % 8) // 2, c % 2
        self.zl, self.y = d // 4, d % 4

    def at(self, x=None, core=None, y=None, zl=None, zh=None):
        x = self.x if x is None else x
        core = self.core if core is None else core
        y = self.y if y is None else y
        zl = self.zl if zl is None else zl
        zh = self.zh if zh is None else zh
        return (zh * 8 + x * 2 + core, zl * 4 + y)


def both(*conds):
    total = conds[0]
    for cond in conds[1:]:
        total = jnp.logical_and(total, cond)
    return total


class Sends:
    def __init__(self, sems):
        self.sems, self.count, self.open = sems, 0, []

    def start(self, cond, src, dst, recv_sem, device):
        copy = pltpu.make_async_remote_copy(
            src_ref=src, dst_ref=dst, send_sem=self.sems.at[self.count], recv_sem=recv_sem,
            device_id=device, device_id_type=MESH,
        )
        self.count += 1
        self.open.append((cond, copy))
        if cond is None:
            copy.start()
        else:
            pl.when(cond)(copy.start)

    def finish(self):
        for cond, copy in self.open:
            if cond is None:
                copy.wait_send()
            else:
                pl.when(cond)(copy.wait_send)
        self.open = []


def arrived(dst, sem):
    pltpu.make_async_copy(dst, dst, sem).wait()


def signal(cond, sem, device):
    def act():
        pl.semaphore_signal(sem, inc=1, device_id=device, device_id_type=MESH)
    if cond is None:
        act()
    else:
        pl.when(cond)(act)


def number(cond):
    return jnp.where(cond, 1, 0).astype(jnp.int32)


def gather_kernel(k_ref, v_ref, kv_ref, rel, ssem, rsem, relsem, lsem):
    p = Place()
    x, core = p.x, p.core
    own = (k_ref, v_ref)
    up, down = (p.zh + 1) % 4, (p.zh + 3) % 4
    owner = jnp.logical_or(x == 3, both(x == 2, core == 1))
    blk = 2 * (x - 2) + core - 1
    owners = ((2, 1, 0), (3, 0, 1), (3, 1, 2))

    bar = pltpu.get_barrier_semaphore()
    signal(None, bar, p.at(core=1 - core))
    for c2 in range(2):
        signal(x >= 1, bar, p.at(x=x - 1, core=c2))
    signal(both(x >= 2, core == 0), bar, p.at(x=x - 2, core=1))
    for ox, oc, b in owners:
        signal(jnp.logical_not(both(x == ox, core == oc)), bar, p.at(x=ox, core=oc))
    for j in range(4):
        signal(x == 0, bar, p.at(x=j, zh=down))
        signal(both(x == 0, core == 0), bar, p.at(x=j, core=1, zh=down))
    peers = 2 + core + 2 * number(x <= 2) + number(both(x <= 1, core == 1)) + 7 * number(owner)
    pl.semaphore_wait(bar, peers)

    def slot(kind, s):
        return kv_ref.at[kind, pl.ds(s * TOK, TOK), :]

    def rs(kind, s):
        return rsem.at[kind, s - 1]

    sends = Sends(ssem)
    for j in range(4):
        for t in range(2):
            mine = both(x == j, core == t)
            piece = own[t].at[:, pl.ds(j * HD, HD)]
            sends.start(both(owner, jnp.logical_not(mine)), piece, rel.at[blk], relsem.at[blk], p.at(x=j, core=t))
            local = pltpu.make_async_copy(piece, rel.at[blk], relsem.at[blk])
            pl.when(both(owner, mine))(local.start)
    for kind in range(2):
        pltpu.make_async_copy(own[kind], slot(kind, 0), lsem.at[kind]).start()
    for kind in range(2):
        s = 2 + kind - core
        sends.start(x <= 2, own[kind], slot(kind, s), rs(kind, s), p.at(x=x + 1, core=kind))
    for kind in range(2):
        sends.start(both(x <= 1, core == 1), own[kind], slot(kind, 3), rs(kind, 3), p.at(x=x + 2, core=0))
    for kind in range(2):
        sends.start(core == 0, own[kind], slot(kind, 1), rs(kind, 1), p.at(core=1))
    lanes = pl.ds(pl.multiple_of(x * HD, HD), HD)

    def part(s):
        return kv_ref.at[core, pl.ds(s * TOK, TOK), lanes]

    for b in range(3):
        arrived(rel.at[b], relsem.at[b])
        s = (3 - b) + (0 if b == 0 else core)
        target = p.at(x=0, zh=up, core=0 if b == 0 else core)
        sends.start(None, rel.at[b], part(s), rsem.at[core, s - 1], target)
    for s in (1, 2):
        pl.when(core == 0)(lambda s=s: arrived(slot(0, s), rs(0, s)))
        pl.when(core == 1)(lambda s=s: arrived(slot(1, s + 1), rs(1, s + 1)))
        sends.start(core == 0, slot(0, s), slot(0, s + 1), rs(0, s + 1), p.at(core=1))
        sends.start(core == 1, slot(1, s + 1), slot(1, s), rs(1, s), p.at(core=0))
        if s == 1:
            sends.start(both(x == 0, core == 0), slot(0, 1), slot(0, 3), rs(0, 3), p.at(x=1, core=0))
            sends.start(both(x == 0, core == 1), slot(1, 2), slot(1, 3), rs(1, 3), p.at(x=1, core=0))

    @pl.when(core == 0)
    def _():
        arrived(slot(0, 3), rs(0, 3))
        for s in (1, 2, 3):
            arrived(slot(1, s), rs(1, s))

    @pl.when(core == 1)
    def _():
        arrived(slot(1, 1), rs(1, 1))
        for s in (1, 2, 3):
            arrived(slot(0, s), rs(0, s))

    for kind in range(2):
        pltpu.make_async_copy(own[kind], slot(kind, 0), lsem.at[kind]).wait()
    sends.finish()


def gather(keys, values):
    return pl.pallas_call(
        gather_kernel,
        out_shape=jax.ShapeDtypeStruct((2, STEPS * TOK, KVH * HD), BF),
        in_specs=[pl.BlockSpec(memory_space=pl.ANY)] * 2,
        out_specs=pl.BlockSpec(memory_space=pl.ANY),
        scratch_shapes=[
            pltpu.VMEM((3, TOK, HD), BF),
            pltpu.SemaphoreType.DMA((24,)),
            pltpu.SemaphoreType.DMA((2, 3)),
            pltpu.SemaphoreType.DMA((3,)),
            pltpu.SemaphoreType.DMA((2,)),
        ],
        compiler_params=pltpu.CompilerParams(collective_id=0, has_side_effects=True),
    )(keys, values)


def attend_kernel(order_ref, q_ref, do_ref, k_ref, v_ref, o_ref, dq_ref, dkv_ref, gram_ref, bias, kt, vt, dk, dv):
    p = pl.program_id(0)
    c = lax.axis_index("ctx")
    half = TOK // 2

    @pl.when(p == 0)
    def _():
        row = lax.broadcasted_iota(jnp.int32, (half, TOK), 0)
        col = lax.broadcasted_iota(jnp.int32, (half, TOK), 1)
        qa, qb = order_ref[2 * c], order_ref[2 * c + 1]
        query_place = jnp.where(col < half, qa * half + col, qb * half + (col - half))
        for s in range(STEPS):
            kc = (c - s + 32) % 32
            for part in range(2):
                key_place = order_ref[2 * kc + part] * half + row
                b = jnp.where(key_place <= query_place, 0.0, NEG).astype(F32)
                rows = pl.ds(s * TOK + part * half, half)
                bias[rows, 0:TOK] = b
                bias[rows, TOK:2 * TOK] = b

    @pl.when(p % 4 == 0)
    def _():
        kt[...] = jnp.transpose(k_ref[0])
        vt[...] = jnp.transpose(v_ref[0])
        dk[...] = jnp.zeros_like(dk)
        dv[...] = jnp.zeros_like(dv)

    q2 = jnp.concatenate([q_ref[:, 0:HD], q_ref[:, HD:2 * HD]], axis=0)
    do2 = jnp.concatenate([do_ref[:, 0:HD], do_ref[:, HD:2 * HD]], axis=0)
    s = dot(k_ref[0], q2, 1, 1) * (SCALE * LOG2E) + bias[...]
    dp = dot(v_ref[0], do2, 1, 1)
    m = jnp.max(s, axis=0, keepdims=True)
    w = jnp.exp2(s - m)
    total = jnp.sum(w, axis=0, keepdims=True)
    mixed = jnp.sum(w * dp, axis=0, keepdims=True)
    inv = 1.0 / total
    delta = mixed * inv
    prob = w * inv
    pb = prob.astype(BF)
    ds = (prob * (dp - delta)).astype(BF)
    ot = dot(vt[...], pb, 1, 0).astype(BF)
    dqt = (dot(kt[...], ds, 1, 0) * SCALE).astype(BF)
    for h in range(2):
        lanes = slice(h * HD, (h + 1) * HD)
        oh = ot[:, h * TOK:(h + 1) * TOK]
        o_ref[:, lanes] = jnp.transpose(oh)
        dq_ref[:, lanes] = jnp.transpose(dqt[:, h * TOK:(h + 1) * TOK])
        gram_ref[h, 0] = dot(oh, oh, 1, 1).astype(BF)
    dv[...] += dot(pb, do2, 1, 0)
    dk[...] += dot(ds, q2, 1, 0)

    @pl.when(p % 4 == 3)
    def _():
        dkv_ref[0] = (dk[...] * SCALE).astype(BF)
        dkv_ref[1] = dv[...].astype(BF)


def attend(order, q, do, kv):
    heads = q.shape[1] // HD
    keys = STEPS * TOK
    return pl.pallas_call(
        attend_kernel,
        grid=(heads // 2,),
        in_specs=[
            pl.BlockSpec(memory_space=pltpu.SMEM),
            pl.BlockSpec((TOK, 2 * HD), lambda p: (0, p)),
            pl.BlockSpec((TOK, 2 * HD), lambda p: (0, p)),
            pl.BlockSpec((1, keys, HD), lambda p: (0, 0, p // 4)),
            pl.BlockSpec((1, keys, HD), lambda p: (1, 0, p // 4)),
        ],
        out_specs=[
            pl.BlockSpec((TOK, 2 * HD), lambda p: (0, p)),
            pl.BlockSpec((TOK, 2 * HD), lambda p: (0, p)),
            pl.BlockSpec((2, keys, HD), lambda p: (0, 0, p // 4)),
            pl.BlockSpec((2, 1, HD, HD), lambda p: (0, p, 0, 0)),
        ],
        out_shape=[
            jax.ShapeDtypeStruct((TOK, heads * HD), BF),
            jax.ShapeDtypeStruct((TOK, heads * HD), BF),
            jax.ShapeDtypeStruct((2, keys, KVH * HD), BF),
            jax.ShapeDtypeStruct((2, heads // 2, HD, HD), BF),
        ],
        scratch_shapes=[
            pltpu.VMEM((keys, 2 * TOK), F32),
            pltpu.VMEM((HD, keys), BF),
            pltpu.VMEM((HD, keys), BF),
            pltpu.VMEM((keys, HD), F32),
            pltpu.VMEM((keys, HD), F32),
        ],
        compiler_params=pltpu.CompilerParams(vmem_limit_bytes=32 * 2**20),
    )(order, q, do, kv, kv)


def reduce_kernel(
    dkv_ref, gram_ref, dk_ref, dv_ref, of_ref, gf_ref,
    mate, snd, rel, in1, in2,
    g0, ay, ry, ax, rx, az, rz, ah, rh,
    zown, zin, cs, cr, xs, xr, ls, lr, fs, fr,
    ssem, msem, relsem, in1sem, in2sem, osem, gsem, lsem,
):
    p = Place()
    x, core, y, zl, zh = p.x, p.core, p.y, p.zl, p.zh
    down = (zh + 3) % 4
    up = (zh + 1) % 4
    other = 1 - core
    bar = pltpu.get_barrier_semaphore()

    def ring(v, j):
        return (v + j) % 4

    for j in range(4):
        for t in range(2):
            signal(jnp.logical_not(both(x == j, core == t)), bar, p.at(x=j, core=t))
    for j in (1, 2, 3):
        signal(None, bar, p.at(y=ring(y, j)))
        signal(None, bar, p.at(zl=ring(zl, j)))
        signal(None, bar, p.at(zh=ring(zh, j)))
    for j in range(4):
        for t in range(2):
            signal(x == 3, bar, p.at(x=j, core=t, zh=up))
            signal(both(x == 2, core == 1), bar, p.at(x=j, core=t, zh=up))
        signal(jnp.logical_not(both(y == zh, zh == j)), bar, p.at(y=zh, zh=j))
    pl.semaphore_wait(bar, 7 + 9 + 3 + 4 - number(y == zh))

    sends = Sends(ssem)
    part = lambda kind, s: dkv_ref.at[kind, pl.ds(s * TOK, TOK), :]

    for i in range(2):
        sends.start(core == 0, part(1, 1 + i), mate.at[i], msem.at[i], p.at(core=1))
        sends.start(core == 1, part(0, 2 + i), mate.at[i], msem.at[i], p.at(core=0))
    for kind in range(2):
        sends.start(core == 1, part(kind, 1), in2.at[kind], in2sem.at[kind], p.at(core=0))
        sends.start(both(core == 0, x >= 2), part(kind, 3), in2.at[kind], in2sem.at[kind], p.at(x=x - 2, core=1))
        for j in range(4):
            piece = dkv_ref.at[kind, pl.ds(3 * TOK, TOK), pl.ds(j * HD, HD)]
            for sx, b in ((0, 2), (1, 3)):
                here = both(core == 0, x == sx)
                if kind == 0 and j == sx:
                    pl.when(here)(pltpu.make_async_copy(piece, rel.at[b], relsem.at[b]).start)
                else:
                    sends.start(here, piece, rel.at[b], relsem.at[b], p.at(x=j, core=kind))
    sends.start(None, gram_ref.at[other], g0, osem.at[0], p.at(core=other))

    for i in range(2):
        arrived(mate.at[i], msem.at[i])
        mine = dkv_ref[core, pl.ds(pl.multiple_of((1 + i + core) * TOK, TOK), TOK), :]
        snd[i] = (mine.astype(F32) + mate[i].astype(F32)).astype(BF)
        sends.start(x >= 1, snd.at[i], in1.at[core], in1sem.at[core], p.at(x=x - 1, core=1 - i))
        for j in range(4):
            piece = snd.at[i, :, pl.ds(j * HD, HD)]
            if j == 0:
                pl.when(x == 0)(pltpu.make_async_copy(piece, rel.at[i], relsem.at[i]).start)
            else:
                sends.start(x == 0, piece, rel.at[i], relsem.at[i], p.at(x=j))
    lanes = pl.ds(pl.multiple_of(x * HD, HD), HD)
    arrived(rel.at[2], relsem.at[2])
    sends.start(None, rel.at[2], in2.at[core, :, lanes], in2sem.at[core], p.at(x=2, core=1, zh=down))
    arrived(rel.at[1], relsem.at[1])
    sends.start(None, rel.at[1], in1.at[core, :, lanes], in1sem.at[core], p.at(x=3, core=0, zh=down))
    arrived(rel.at[0], relsem.at[0])
    arrived(rel.at[3], relsem.at[3])
    rel[4] = (rel[0].astype(F32) + rel[3].astype(F32)).astype(BF)
    sends.start(None, rel.at[4], in1.at[core, :, lanes], in1sem.at[core], p.at(x=3, core=1, zh=down))

    arrived(g0, osem.at[0])

    def rows_of_y(h, _):
        both_cores = gram_ref[core, h].astype(F32) + g0[h].astype(F32)
        split = both_cores.reshape(4, 4, 8, HD)
        for j in range(4):
            ay[j, pl.ds(pl.multiple_of(h * 32, 32), 32), :] = split[:, j].reshape(32, HD).astype(BF)
        return 0

    lax.fori_loop(0, 16, rows_of_y, 0)
    for j in (1, 2, 3):
        sends.start(None, ay.at[ring(y, j)], ry.at[j - 1], osem.at[j], p.at(y=ring(y, j)))
    for j in (1, 2, 3):
        arrived(ry.at[j - 1], osem.at[j])

    def heads_of_x(h, _):
        rows = pl.ds(pl.multiple_of(h * 32, 32), 32)
        total = ay[y, rows, :].astype(F32)
        for j in range(3):
            total = total + ry[j, rows, :].astype(F32)
        ax[h % 4, pl.ds(pl.multiple_of((h // 4) * 32, 32), 32), :] = total.astype(BF)
        return 0

    lax.fori_loop(0, 16, heads_of_x, 0)
    for j in (1, 2, 3):
        sends.start(None, ax.at[ring(x, j)], rx.at[j - 1], osem.at[3 + j], p.at(x=ring(x, j)))
    for j in (1, 2, 3):
        arrived(rx.at[j - 1], osem.at[3 + j])
    total = ax[x].astype(F32)
    for j in range(3):
        total = total + rx[j].astype(F32)
    total = total.reshape(4, 4, 8, HD)
    for j in range(4):
        az[j] = total[:, j]
    for j in (1, 2, 3):
        sends.start(None, az.at[ring(zl, j)], rz.at[j - 1], osem.at[6 + j], p.at(zl=ring(zl, j)))
    for j in (1, 2, 3):
        arrived(rz.at[j - 1], osem.at[6 + j])
    ah[...] = az[zl] + rz[0] + rz[1] + rz[2]
    for j in (1, 2, 3):
        sends.start(None, ah.at[ring(zh, j)], rh.at[j - 1], osem.at[9 + j], p.at(zh=ring(zh, j)))

    for kind in range(2):
        arrived(in1.at[kind], in1sem.at[kind])
    last = both(x == 3, core == 1)
    outs = (dk_ref, dv_ref)
    for kind in range(2):
        near = dkv_ref[kind, pl.ds(0, TOK), :].astype(F32) + in1[kind].astype(F32)

        @pl.when(last)
        def _():
            outs[kind][0] = near.astype(BF)

        @pl.when(jnp.logical_not(last))
        def _():
            arrived(in2.at[kind], in2sem.at[kind])
            outs[kind][0] = (near + in2[kind].astype(F32)).astype(BF)

    for g in range(KVH):
        for kind in range(2):
            zown[g, :, pl.ds(kind * HD, HD)] = outs[kind][0, :, pl.ds(g * HD, HD)]
    for j in (1, 2, 3):
        sends.start(None, zown.at[ring(y, j)], zin.at[j - 1], gsem.at[j - 1], p.at(y=ring(y, j)))
    gram = dot(zown[y], zown[y], 0, 0)
    for j in (1, 2, 3):
        arrived(zin.at[j - 1], gsem.at[j - 1])
        z = zin[j - 1]
        gram = gram + dot(z, z, 0, 0)
    gram = gram.reshape(4, 2, 32, 2 * HD)
    for c2 in range(2):
        cs[c2] = gram[:, c2].astype(BF)
    sends.start(None, cs.at[other], cr, gsem.at[3], p.at(core=other))
    arrived(cr, gsem.at[3])
    xs[...] = (cs[core].astype(F32) + cr[...].astype(F32)).astype(BF)
    for j in (1, 2, 3):
        sends.start(None, xs.at[ring(x, j)], xr.at[j - 1], gsem.at[3 + j], p.at(x=ring(x, j)))
    total = xs[x].astype(F32)
    for j in (1, 2, 3):
        arrived(xr.at[j - 1], gsem.at[3 + j])
        total = total + xr[j - 1].astype(F32)
    ls[...] = total.reshape(4, 8, 2 * HD)
    for j in (1, 2, 3):
        sends.start(None, ls.at[ring(zl, j)], lr.at[j - 1], gsem.at[6 + j], p.at(zl=ring(zl, j)))
    total = ls[zl]
    for j in (1, 2, 3):
        arrived(lr.at[j - 1], gsem.at[6 + j])
        total = total + lr[j - 1]
    for j in range(4):
        fs[j] = total[2 * j:2 * j + 2, :]
    for j in range(4):
        away = jnp.logical_not(both(y == j, zh == y))
        sends.start(away, fs.at[j], fr.at[zh], gsem.at[10 + zh], p.at(y=j, zh=y))
        pl.when(both(y == j, zh == y))(
            pltpu.make_async_copy(fs.at[j], fr.at[zh], gsem.at[10 + zh]).start)
    tokens = float(512 * TOK)
    for j in (1, 2, 3):
        arrived(rh.at[j - 1], osem.at[9 + j])
    of_ref[...] = (ah[zh] + rh[0] + rh[1] + rh[2]) / tokens
    for j in range(4):
        arrived(fr.at[j], gsem.at[10 + j])
    gf_ref[...] = (fr[0] + fr[1] + fr[2] + fr[3]) / tokens
    sends.finish()


def reduce(dkv, gram):
    vmem = pl.BlockSpec(memory_space=pltpu.VMEM)
    wide = KVH * HD
    return pl.pallas_call(
        reduce_kernel,
        out_shape=[
            jax.ShapeDtypeStruct((1, TOK, wide), BF),
            jax.ShapeDtypeStruct((1, TOK, wide), BF),
            jax.ShapeDtypeStruct((8, HD), F32),
            jax.ShapeDtypeStruct((2, 2 * HD), F32),
        ],
        in_specs=[vmem, vmem],
        out_specs=[vmem] * 4,
        scratch_shapes=[
            pltpu.VMEM((2, TOK, wide), BF),
            pltpu.VMEM((2, TOK, wide), BF),
            pltpu.VMEM((5, TOK, HD), BF),
            pltpu.VMEM((2, TOK, wide), BF),
            pltpu.VMEM((2, TOK, wide), BF),
            pltpu.VMEM((16, HD, HD), BF),
            pltpu.VMEM((4, 512, HD), BF),
            pltpu.VMEM((3, 512, HD), BF),
            pltpu.VMEM((4, 128, HD), BF),
            pltpu.VMEM((3, 128, HD), BF),
            pltpu.VMEM((4, 4, 8, HD), F32),
            pltpu.VMEM((3, 4, 8, HD), F32),
            pltpu.VMEM((4, 8, HD), F32),
            pltpu.VMEM((3, 8, HD), F32),
            pltpu.VMEM((4, TOK, 2 * HD), BF),
            pltpu.VMEM((3, TOK, 2 * HD), BF),
            pltpu.VMEM((2, 4, 32, 2 * HD), BF),
            pltpu.VMEM((4, 32, 2 * HD), BF),
            pltpu.VMEM((4, 32, 2 * HD), BF),
            pltpu.VMEM((3, 32, 2 * HD), BF),
            pltpu.VMEM((4, 8, 2 * HD), F32),
            pltpu.VMEM((3, 8, 2 * HD), F32),
            pltpu.VMEM((4, 2, 2 * HD), F32),
            pltpu.VMEM((4, 2, 2 * HD), F32),
            pltpu.SemaphoreType.DMA((72,)),
            pltpu.SemaphoreType.DMA((2,)),
            pltpu.SemaphoreType.DMA((4,)),
            pltpu.SemaphoreType.DMA((2,)),
            pltpu.SemaphoreType.DMA((2,)),
            pltpu.SemaphoreType.DMA((13,)),
            pltpu.SemaphoreType.DMA((14,)),
            pltpu.SemaphoreType.DMA((2,)),
        ],
        compiler_params=pltpu.CompilerParams(
            collective_id=1, has_side_effects=True, vmem_limit_bytes=32 * 2**20),
    )(dkv, gram)


def local(queries, key_heads, value_heads, out_grad, block_order):
    kv = gather(key_heads[0], value_heads[0])
    attn, dq, dkv, gram = attend(block_order, queries[0], out_grad[0], kv)
    dk, dv, out_factor, grad_factor = reduce(dkv, gram)
    return attn[None], dq[None], dk, dv, out_factor, grad_factor


def solution(mesh):
    rows = P("dp", "ctx", None)
    return jax.shard_map(
        local,
        mesh=mesh,
        in_specs=(rows, rows, rows, rows, P()),
        out_specs=(rows, rows, rows, rows, P(("ctx", "dp"), None), P(("ctx", "dp"), None)),
        check_vma=False,
    )
```

time: 657 us -> 111 us (0.17)
  waiting for transfers between devices: 554 us -> 0 us
  Pallas kernels: 0 us -> 105 us
  starting transfers between devices: 43 us -> 0 us
  matrix products: 19.9 us -> 0 us
  between operations: 14.8 us -> 0.69 us
  local copies, waits for them, and re-layouts: 15.6 us -> 4.93 us
  other arithmetic: 8.05 us -> 0 us
    unnamed x2 -> x0, waiting for transfers between devices: 490 us -> none
    pallas_call x0 -> x3, Pallas kernels: none -> 105 us  [the longest x1 55.6 us: reduce(): pl.pallas_call(reduce_kernel, out_shape=[jax.ShapeDtypeStruct((1, TOK, wi...]
    ppermute x14 -> x0, waiting for transfers between devices: 63.4 us -> none  [from_behind(): lax.ppermute(value, axis, [(i, (i + by) % size) for i in range(size)])]
    ppermute x14 -> x0, starting transfers between devices: 43 us -> none  [from_behind(): lax.ppermute(value, axis, [(i, (i + by) % size) for i in range(size)])]
    dot_general x26 -> x0, matrix products: 19.9 us -> none  [the longest x4 3.94 us: local(): jnp.einsum('tgjd,ugd->gjtu', grad_local, value_block, preferred_element_t...]
    unnamed x62 -> x12, local copies, waits for them, and re-layouts: 14.2 us -> 4.93 us
  transfers between devices with their start and end apart: 15 -> 0, of which waited for: 8 -> 0; matrix products, arithmetic and copies ran while one was open for 5% -> 0% of each run, Pallas kernels for 0% -> 0%
where the time goes in v1:
time: 111 us; the launch traced here: 110 us
  Pallas kernels  105 us (95%)
  local copies, waits for them, and re-layouts  4.93 us (4%)
    pallas_call x1, Pallas kernels, reduce(): pl.pallas_call(reduce_kernel, out_shape=[jax.ShapeDtypeStruct((1, TOK, wi...  55.6 us
    pallas_call x1, Pallas kernels, gather(): pl.pallas_call(gather_kernel, out_shape=jax.ShapeDtypeStruct((2, STEPS *...  28.5 us
    pallas_call x1, Pallas kernels, attend(): pl.pallas_call(attend_kernel, grid=(heads // 2,), in_specs=[pl.BlockSpec(...  20.5 us
    unnamed x12, local copies, waits for them, and re-layouts  4.93 us

profile of v1, /device:TPU:1, one launch (start us, length us, event | category | flops | bytes accessed | tf_op | source)
XLA Modules:
  0.0 110.2 jit_solution(11179778080295108351)
XLA Ops:
  0.6 0.0 copy-start.1
  0.6 0.0 copy-start.3
  0.7 28.5 %shard_map.100.k_ref.v_ref = bf16[2,512,512]{2,1,0:T(8,128)(2,1)} custom-call(bf16[128,512]{1,0:T(8,128)(2,1)} %bitcast.8, bf16[128,512]{1,0:T(8,128)(2,1)} %bitcast.9), custom_call_target="tpu_custom_call" | custom-call | tf_op jit(solution)/shard_map/pallas_call | solution.py:172
  29.2 0.0 copy-done.1
  29.2 0.0 copy-done.3
  29.2 0.0 copy-start
  29.2 1.2 %copy-done = bf16[2,512,512]{2,1,0:T(8,128)(2,1)S(1)} copy-done((bf16[2,512,512]{2,1,0:T(8,128)(2,1)S(1)}, bf16[2,512,512]{2,1,0:T(8,128)(2,1)}, u32[]{:S(2)}) %copy-start) | copy-done | bytes 1048600
  30.4 0.0 copy-start.2
  30.4 1.2 %copy-done.2 = bf16[1,128,4096]{2,1,0:T(8,128)(2,1)S(1)} copy-done((bf16[1,128,4096]{2,1,0:T(8,128)(2,1)S(1)}, bf16[1,128,4096]{2,1,0:T(8,128)(2,1)}, u32[]{:S(2)}) %copy-start.2) | copy-done | bytes 1048600
  31.6 20.5 %shard_map.101 = (bf16[128,4096]{1,0:T(8,128)(2,1)}, bf16[128,4096]{1,0:T(8,128)(2,1)}, bf16[2,512,512]{2,1,0:T(8,128)(2,1)S(1)}, bf16[2,16,128,128]{3,2,1,0:T(8,128)(2,1)S(1)}) custom-call(s32[64]{0:T(128)S(1)} %copy-done.3, bf16[128,4096]{1,0:T(8,128)(2,1)S(1)} %bitcast.6, bf16[128,4096]{1,0:T(8,128)(2,1)S(1)} %bitcast.7, ...), custom_call_target="tpu_custom_call" | custom-call | tf_op jit(solution)/shard_map/pallas_call | solution.py:248
  52.2 55.6 %shard_map.102 = (bf16[1,128,512]{2,1,0:T(8,128)(2,1)S(1)}, bf16[1,128,512]{2,1,0:T(8,128)(2,1)S(1)}, f32[8,128]{1,0:T(8,128)S(1)}, f32[2,256]{1,0:T(2,128)S(1)}) custom-call(bf16[2,512,512]{2,1,0:T(8,128)(2,1)S(1)} %get-tuple-element.16.dkv_ref, bf16[2,16,128,128]{3,2,1,0:T(8,128)(2,1)S(1)} %get-tuple-element.17.gram_ref), custom_call_target="tpu_custom_call" | custom-call | tf_op jit(solution)/shard_map/pallas_call | solution.py:459
  107.8 0.7 copy.15
  108.4 0.7 copy.16
  109.1 0.6 copy.17
  109.7 0.6 copy.18
Async XLA Ops:
  0.6 28.5 %copy-start.1 = (bf16[1,128,4096]{2,1,0:T(8,128)(2,1)S(1)}, bf16[1,128,4096]{2,1,0:T(8,128)(2,1)}, u32[]{:S(2)}) copy-start(bf16[1,128,4096]{2,1,0:T(8,128)(2,1)} %param.5) | copy-start | bytes 3145732
  0.6 28.5 %copy-start.3 = (s32[64]{0:T(128)S(1)}, s32[64]{0:T(128)}, u32[]{:S(2)}) copy-start(s32[64]{0:T(128)} %order_ref.1) | copy-start | bytes 772
  29.2 1.2 %copy-start = (bf16[2,512,512]{2,1,0:T(8,128)(2,1)S(1)}, bf16[2,512,512]{2,1,0:T(8,128)(2,1)}, u32[]{:S(2)}) copy-start(bf16[2,512,512]{2,1,0:T(8,128)(2,1)} %shard_map.100.k_ref.v_ref) | copy-start | bytes 3145732
  30.4 1.2 %copy-start.2 = (bf16[1,128,4096]{2,1,0:T(8,128)(2,1)S(1)}, bf16[1,128,4096]{2,1,0:T(8,128)(2,1)}, u32[]{:S(2)}) copy-start(bf16[1,128,4096]{2,1,0:T(8,128)(2,1)} %param.8) | copy-start | bytes 3145732

commit v2 on v0

v2 whole, which is shorter than its diff:
```python
import math

import jax
import jax.numpy as jnp
from jax import lax
from jax.experimental import pallas as pl
from jax.experimental.pallas import tpu as pltpu
from jax.sharding import PartitionSpec as P

HD = 128
STEPS = 4
TOK = 128
QUARTER = TOK // 4
KVH = 4
NEG = -1e30
LOG2E = 1.0 / math.log(2.0)
SCALE = 1.0 / math.sqrt(HD)
MESH = pl.DeviceIdType.MESH
BF = jnp.bfloat16
F32 = jnp.float32


def dot(a, b, ca, cb):
    return lax.dot_general(a, b, (((ca,), (cb,)), ((), ())), preferred_element_type=F32)


class Place:
    def __init__(self):
        c, d = lax.axis_index("ctx"), lax.axis_index("dp")
        self.zh, self.x, self.core = c // 8, (c % 8) // 2, c % 2
        self.zl, self.y = d // 4, d % 4

    def at(self, x=None, core=None, y=None, zl=None, zh=None):
        x = self.x if x is None else x
        core = self.core if core is None else core
        y = self.y if y is None else y
        zl = self.zl if zl is None else zl
        zh = self.zh if zh is None else zh
        return (zh * 8 + x * 2 + core, zl * 4 + y)


def both(*conds):
    total = conds[0]
    for cond in conds[1:]:
        total = jnp.logical_and(total, cond)
    return total


class Sends:
    def __init__(self, sems):
        self.sems, self.keys = sems, {}

    def start(self, key, cond, src, dst, recv_sem, device, whole):
        if key not in self.keys:
            self.keys[key] = (len(self.keys), cond, whole)
        copy = pltpu.make_async_remote_copy(
            src_ref=src, dst_ref=dst, send_sem=self.sems.at[self.keys[key][0]], recv_sem=recv_sem,
            device_id=device, device_id_type=MESH,
        )
        if cond is None:
            copy.start()
        else:
            pl.when(cond)(copy.start)

    def finish(self):
        for index, cond, whole in self.keys.values():
            def act(index=index, whole=whole):
                arrived(whole, self.sems.at[index])
            if cond is None:
                act()
            else:
                pl.when(cond)(act)


def arrived(dst, sem):
    pltpu.make_async_copy(dst, dst, sem).wait()


def local_copy(cond, src, dst, sem):
    copy = pltpu.make_async_copy(src, dst, sem)
    if cond is None:
        copy.start()
    else:
        pl.when(cond)(copy.start)


def signal(cond, sem, device):
    def act():
        pl.semaphore_signal(sem, inc=1, device_id=device, device_id_type=MESH)
    if cond is None:
        act()
    else:
        pl.when(cond)(act)


def number(cond):
    return jnp.where(cond, 1, 0).astype(jnp.int32)


def lanes_of(g, count=1):
    if isinstance(g, int):
        return pl.ds(g * HD, count * HD)
    return pl.ds(pl.multiple_of(g * HD, HD), count * HD)


def rows_of(j):
    return pl.ds(pl.multiple_of(j * QUARTER, QUARTER), QUARTER)


def ring(v, j):
    return (v + j) % 4


def fused_kernel(
    order_ref, q_hbm, do_hbm, k_hbm, v_hbm,
    attn_hbm, dq_hbm, dk_ref, dv_ref, of_ref, gf_ref,
    qv, dov, ov, dqv, kvs, dkv, gram, bias,
    rel, mate, snd, rel2, relsum, in1, in2,
    g0, ay, ry, ax, rx, az, rz, ah, rh,
    zown, zin, cs, cr, xs, xr, ls, lr, fs, fr,
    ssem, qsem, outsem, ownsem, rsem, relsem, msem, rel2sem, in1sem, in2sem,
    o0sem, oysem, oxsem, ozsem, gsem, ready2, ready3,
):
    p = Place()
    x, core, y, zl, zh = p.x, p.core, p.y, p.zl, p.zh
    up, down, other = ring(zh, 1), ring(zh, 3), 1 - core
    own = (k_hbm, v_hbm)
    owner = jnp.logical_or(x == 3, both(x == 2, core == 1))
    blk = 2 * (x - 2) + core - 1
    bar = pltpu.get_barrier_semaphore()
    sends = Sends(ssem)

    core0, core1 = core == 0, core == 1
    x0, x_up, x0core0, x0core1 = x == 0, x >= 1, both(x == 0, core == 0), both(x == 0, core == 1)
    tail_at = {0: x0core0, 1: both(x == 1, core == 0)}
    two_up = both(core == 0, x >= 2)
    elsewhere = [y != g for g in range(KVH)]
    tall, thin, one_slot = mate.at[0], rel2.at[0], kvs.at[0, :, pl.ds(0, TOK), :]
    one_ay, one_ax, one_z = ay.at[0], ax.at[0], zown.at[0]

    signal(None, bar, p.at(zh=up))
    signal(None, bar, p.at(zh=down))
    for j in range(4):
        signal(x == 0, bar, p.at(x=j, zh=down))
        signal(both(x == 0, core == 0), bar, p.at(x=j, core=1, zh=down))
        for t in range(2):
            signal(x == 3, bar, p.at(x=j, core=t, zh=up))
            signal(both(x == 2, core == 1), bar, p.at(x=j, core=t, zh=up))
    for j in (1, 2, 3):
        signal(None, bar, p.at(zl=ring(zl, j)))
        signal(None, bar, p.at(y=ring(y, j)))
    for j in range(4):
        for t in range(2):
            signal(jnp.logical_not(both(x == j, core == t)), bar, p.at(x=j, core=t))

    for g in range(KVH):
        heads = lanes_of(8 * g, 8)
        local_copy(None, q_hbm.at[:, heads], qv.at[:, heads], qsem.at[0, g])
        local_copy(None, do_hbm.at[:, heads], dov.at[:, heads], qsem.at[1, g])
        if g == 0:
            for kind in range(2):
                for i in range(KVH):
                    local_copy(None, own[kind].at[:, lanes_of(i)], kvs.at[kind, i, pl.ds(0, TOK), :], ownsem.at[kind])
    half = TOK // 2
    c = lax.axis_index("ctx")
    row = lax.broadcasted_iota(jnp.int32, (half, TOK), 0)
    col = lax.broadcasted_iota(jnp.int32, (half, TOK), 1)
    query_place = jnp.where(col < half, order_ref[2 * c] * half + col, order_ref[2 * c + 1] * half + (col - half))
    for s in range(STEPS):
        kc = (c - s + 32) % 32
        for part in range(2):
            key_place = order_ref[2 * kc + part] * half + row
            bias[pl.ds(s * TOK + part * half, half), :] = jnp.where(key_place <= query_place, 0.0, NEG).astype(F32)
    pl.semaphore_wait(bar, 7 + 3 + 3 + 2 + 1 + core + 3)

    def slot(kind, s, g):
        return kvs.at[kind, g, pl.ds(s * TOK, TOK), :]

    for kind in range(2):
        arrived(kvs.at[kind, :, pl.ds(0, TOK), :], ownsem.at[kind])

    for wide in range(2):
        group = pl.ds(0, 1) if wide == 0 else pl.ds(1, 3)
        for j in range(4):
            for t in range(2):
                mine = both(x == j, core == t)
                piece = kvs.at[t, group, pl.ds(j * QUARTER, QUARTER), :]
                target = rel.at[blk, group]
                sends.start(("spread", j, t), both(owner, jnp.logical_not(mine)), piece, target,
                            relsem.at[blk, wide], p.at(x=j, core=t), rel.at[0])
                local_copy(both(owner, mine), piece, target, relsem.at[blk, wide])
    for g in range(KVH):
        for kind in range(2):
            piece = slot(kind, 0, g)
            s = 2 + kind - core
            sends.start(("near", kind), x <= 2, piece, slot(kind, s, g), rsem.at[kind, s - 1, g],
                        p.at(x=x + 1, core=kind), one_slot)
            sends.start(("far", kind), both(x <= 1, core == 1), piece, slot(kind, 3, g), rsem.at[kind, 2, g],
                        p.at(x=x + 2, core=0), one_slot)
            sends.start(("own", kind), core == 0, piece, slot(kind, 1, g), rsem.at[kind, 0, g],
                        p.at(core=1), one_slot)
        if g == 0:
            relay_in(rel, relsem, 0)
            relay_out(sends, p, rel, kvs, rsem, 0, up)
    relay_in(rel, relsem, 1)
    for g in range(1, KVH):
        relay_out(sends, p, rel, kvs, rsem, g, up)
    for side in (up, down):
        signal(None, ready2, p.at(zh=side))

    def forward(g):
        for s in (1, 2):
            pl.when(core == 0)(lambda: arrived(slot(0, s, g), rsem.at[0, s - 1, g]))
            pl.when(core == 1)(lambda: arrived(slot(1, s + 1, g), rsem.at[1, s, g]))
            sends.start(("fk", s), core0, slot(0, s, g), slot(0, s + 1, g), rsem.at[0, s, g],
                        p.at(core=1), one_slot)
            sends.start(("fv", s), core1, slot(1, s + 1, g), slot(1, s, g), rsem.at[1, s - 1, g],
                        p.at(core=0), one_slot)
            if s == 1:
                sends.start(("f3k",), x0core0, slot(0, 1, g), slot(0, 3, g), rsem.at[0, 2, g],
                            p.at(x=1, core=0), one_slot)
                sends.start(("f3v",), x0core1, slot(1, 2, g), slot(1, 3, g), rsem.at[1, 2, g],
                            p.at(x=1, core=0), one_slot)

    def slots_ready(g):
        @pl.when(core == 0)
        def _():
            arrived(slot(0, 3, g), rsem.at[0, 2, g])
            for s in (1, 2, 3):
                arrived(slot(1, s, g), rsem.at[1, s - 1, g])

        @pl.when(core == 1)
        def _():
            arrived(slot(1, 1, g), rsem.at[1, 0, g])
            for s in (1, 2, 3):
                arrived(slot(0, s, g), rsem.at[0, s - 1, g])

    def compute(g):
        keys = kvs[0, g]
        values = kvs[1, g]
        q_all = jnp.concatenate([qv[:, lanes_of(8 * g + h)] for h in range(8)], axis=0)
        do_all = jnp.concatenate([dov[:, lanes_of(8 * g + h)] for h in range(8)], axis=0)
        mask = jnp.concatenate([bias[...], bias[...]], axis=1)
        probs, dscores = [], []
        for pair in range(4):
            cut = slice(pair * 2 * TOK, (pair + 1) * 2 * TOK)
            s = dot(keys, q_all[cut], 1, 1) * (SCALE * LOG2E) + mask
            dp = dot(values, do_all[cut], 1, 1)
            m = jnp.max(s, axis=0, keepdims=True)
            w = jnp.exp2(s - m)
            total = jnp.sum(w, axis=0, keepdims=True)
            mixed = jnp.sum(w * dp, axis=0, keepdims=True)
            inv = 1.0 / total
            delta = mixed * inv
            prob = w * inv
            probs.append(prob.astype(BF))
            dscores.append((prob * (dp - delta)).astype(BF))
        pb = jnp.concatenate(probs, axis=1)
        ds = jnp.concatenate(dscores, axis=1)
        dkv[1, g] = dot(pb, do_all, 1, 0).astype(BF)
        dkv[0, g] = (dot(ds, q_all, 1, 0) * SCALE).astype(BF)
        ot = dot(jnp.transpose(values), pb, 1, 0).astype(BF)
        dqt = (dot(jnp.transpose(keys), ds, 1, 0) * SCALE).astype(BF)
        for h in range(8):
            oh = ot[:, h * TOK:(h + 1) * TOK]
            ov[:, lanes_of(8 * g + h)] = jnp.transpose(oh)
            dqv[:, lanes_of(8 * g + h)] = jnp.transpose(dqt[:, h * TOK:(h + 1) * TOK])
            gram[h % 2, 4 * g + h // 2] = dot(oh, oh, 1, 1).astype(BF)
        heads = lanes_of(8 * g, 8)
        local_copy(None, ov.at[:, heads], attn_hbm.at[:, heads], outsem.at[0])
        local_copy(None, dqv.at[:, heads], dq_hbm.at[:, heads], outsem.at[1])

    def part(kind, s, g):
        return dkv.at[kind, g, pl.ds(s * TOK, TOK), :]

    def home1(g):
        for i in range(2):
            sends.start(("mv", i), core0, part(1, 1 + i, g), mate.at[i, g], msem.at[i, g], p.at(core=1), tall)
            sends.start(("mk", i), core1, part(0, 2 + i, g), mate.at[i, g], msem.at[i, g], p.at(core=0), tall)
        for kind in range(2):
            for j in range(4):
                piece = dkv.at[kind, g, pl.ds(3 * TOK + j * QUARTER, QUARTER), :]
                for sx, b in ((0, 2), (1, 3)):
                    here = tail_at[sx]
                    if kind == 0 and j == sx:
                        local_copy(here, piece, rel2.at[b, g], rel2sem.at[b, g])
                    else:
                        sends.start(("r3", kind, j, b), here, piece, rel2.at[b, g], rel2sem.at[b, g],
                                    p.at(x=j, core=kind), thin)
            sends.start(("m1", kind), core1, part(kind, 1, g), in2.at[kind, g], in2sem.at[kind, g], p.at(core=0), tall)
            sends.start(("m3", kind), two_up, part(kind, 3, g), in2.at[kind, g],
                        in2sem.at[kind, g], p.at(x=x - 2, core=1), tall)

    def home2(g):
        for i in range(2):
            arrived(mate.at[i, g], msem.at[i, g])
            rows = pl.ds(pl.multiple_of((1 + i + core) * TOK, TOK), TOK)
            mine = dkv[core, g, rows, :]
            snd[i, g] = (mine.astype(F32) + mate[i, g].astype(F32)).astype(BF)
            sends.start(("n", i), x_up, snd.at[i, g], in1.at[core, g], in1sem.at[core, g],
                        p.at(x=x - 1, core=1 - i), tall)
            for j in range(4):
                piece = snd.at[i, g, pl.ds(j * QUARTER, QUARTER), :]
                if j == 0:
                    local_copy(x0, piece, rel2.at[i, g], rel2sem.at[i, g])
                else:
                    sends.start(("r", i, j), x0, piece, rel2.at[i, g], rel2sem.at[i, g], p.at(x=j), thin)

    def home3(g):
        def there(ref):
            return ref.at[core, g, rows_of(x), :]

        arrived(rel2.at[2, g], rel2sem.at[2, g])
        sends.start(("h2",), None, rel2.at[2, g], there(in2), in2sem.at[core, g], p.at(x=2, core=1, zh=down), thin)
        arrived(rel2.at[1, g], rel2sem.at[1, g])
        sends.start(("h1",), None, rel2.at[1, g], there(in1), in1sem.at[core, g], p.at(x=3, core=0, zh=down), thin)
        arrived(rel2.at[0, g], rel2sem.at[0, g])
        arrived(rel2.at[3, g], rel2sem.at[3, g])
        relsum[g] = (
            rel2[0, g].astype(F32) + rel2[3, g].astype(F32)).astype(BF)
        sends.start(("h0",), None, relsum.at[g], there(in1), in1sem.at[core, g], p.at(x=3, core=1, zh=down), thin)

    last = both(x == 3, core == 1)
    outs = (dk_ref, dv_ref)

    def home4(g):
        for kind in range(2):
            arrived(in1.at[kind, g], in1sem.at[kind, g])
            near = dkv[kind, g, pl.ds(0, TOK), :].astype(F32) + in1[kind, g].astype(F32)

            @pl.when(last)
            def _():
                outs[kind][0, :, lanes_of(g)] = near.astype(BF)

            @pl.when(jnp.logical_not(last))
            def _():
                arrived(in2.at[kind, g], in2sem.at[kind, g])
                outs[kind][0, :, lanes_of(g)] = (near + in2[kind, g].astype(F32)).astype(BF)

            zown[g, :, pl.ds(kind * HD, HD)] = outs[kind][0, :, lanes_of(g)]
        at = ring(y, 7 - g)
        sends.start(("z", g), elsewhere[g], zown.at[g], zin.at[at], gsem.at[at], p.at(y=g), one_z)

    def out1(g):
        mine = pl.ds(4 * g, 4)
        sends.start(("oc",), None, gram.at[other, mine], g0.at[mine], o0sem.at[g], p.at(core=other), g0)

    def out2(g):
        arrived(g0.at[pl.ds(4 * g, 4)], o0sem.at[g])
        for h in range(4):
            pair_sum = gram[core, 4 * g + h].astype(F32) + g0[4 * g + h].astype(F32)
            split = pair_sum.reshape(4, 4, 8, HD)
            for j in range(4):
                ay[g, j, pl.ds(h * 32, 32), :] = split[:, j].reshape(32, HD).astype(BF)
        for j in (1, 2, 3):
            sends.start(("oy", j), None, ay.at[g, ring(y, j)], ry.at[g, j - 1], oysem.at[g, j - 1], p.at(y=ring(y, j)), one_ay)

    def out3(g):
        for j in range(3):
            arrived(ry.at[g, j], oysem.at[g, j])
        total = ay[g, y].astype(F32)
        for j in range(3):
            total = total + ry[g, j].astype(F32)
        ax[g] = total.reshape(4, 32, HD).astype(BF)
        for j in (1, 2, 3):
            sends.start(("ox", j), None, ax.at[g, ring(x, j)], rx.at[g, j - 1], oxsem.at[g, j - 1], p.at(x=ring(x, j)), one_ax)

    def out4(g):
        for j in range(3):
            arrived(rx.at[g, j], oxsem.at[g, j])
        total = ax[g, x].astype(F32)
        for j in range(3):
            total = total + rx[g, j].astype(F32)
        total = total.reshape(4, 8, HD)
        for j in range(4):
            az[j, g] = total[j]

    forward(0)

    def step(g, _):
        pl.when(g < 3)(lambda: forward(jnp.minimum(g + 1, 3)))
        slots_ready(g)
        heads = lanes_of(8 * g, 8)
        arrived(qv.at[:, heads], qsem.at[0, g])
        arrived(dov.at[:, heads], qsem.at[1, g])
        compute(g)
        home1(g)
        out1(g)

        @pl.when(g >= 1)
        def _():
            home2(g - 1)
            out2(g - 1)

        @pl.when(g >= 2)
        def _():
            home3(g - 2)
            out3(g - 2)

        @pl.when(g == 3)
        def _():
            home4(0)
            out4(0)
        return 0

    lax.fori_loop(0, KVH, step, 0)
    home2(3)
    home3(2)
    out2(3)
    out3(2)
    home4(1)
    out4(1)
    home3(3)
    out3(3)
    home4(2)
    out4(2)
    pl.semaphore_wait(ready2, 2)
    for j in (1, 2, 3):
        signal(None, ready3, p.at(y=ring(y, j)))
    out4(3)
    for j in (1, 2, 3):
        sends.start(("oz", j), None, az.at[ring(zl, j)], rz.at[j - 1], ozsem.at[j - 1], p.at(zl=ring(zl, j)), rz.at[0])
    home4(3)
    for j in range(3):
        arrived(rz.at[j], ozsem.at[j])
    ah[...] = az[zl] + rz[0] + rz[1] + rz[2]
    for j in (1, 2, 3):
        sends.start(("oh", j), None, ah.at[ring(zh, j)], rh.at[j - 1], ozsem.at[2 + j], p.at(zh=ring(zh, j)), rh.at[0])

    mine = zown[y]
    total = dot(mine, mine, 0, 0)
    for j in range(3):
        arrived(zin.at[j], gsem.at[j])
        z = zin[j]
        total = total + dot(z, z, 0, 0)
    total = total.reshape(4, 2, 32, 2 * HD)
    for c2 in range(2):
        cs[c2] = total[:, c2].astype(BF)
    sends.start(("gc",), None, cs.at[other], cr, gsem.at[3], p.at(core=other), cr)
    arrived(cr, gsem.at[3])
    xs[...] = (cs[core].astype(F32) + cr[...].astype(F32)).astype(BF)
    for j in (1, 2, 3):
        sends.start(("gx", j), None, xs.at[ring(x, j)], xr.at[j - 1], gsem.at[3 + j], p.at(x=ring(x, j)), xr.at[0])
    total = xs[x].astype(F32)
    for j in range(3):
        arrived(xr.at[j], gsem.at[4 + j])
        total = total + xr[j].astype(F32)
    ls[...] = total.reshape(4, 8, 2 * HD)
    for j in (1, 2, 3):
        sends.start(("gz", j), None, ls.at[ring(zl, j)], lr.at[j - 1], gsem.at[6 + j], p.at(zl=ring(zl, j)), lr.at[0])
    pl.semaphore_wait(ready3, 3)
    total = ls[zl]
    for j in range(3):
        arrived(lr.at[j], gsem.at[7 + j])
        total = total + lr[j]
    for j in range(4):
        fs[j] = total[2 * j:2 * j + 2, :]
    for j in range(4):
        mine = both(y == j, zh == y)
        sends.start(("gf", j), jnp.logical_not(mine), fs.at[j], fr.at[zh], gsem.at[10 + zh], p.at(y=j, zh=y), fr.at[0])
        local_copy(mine, fs.at[j], fr.at[zh], gsem.at[10 + zh])
    tokens = float(512 * TOK)
    for j in range(3):
        arrived(rh.at[j], ozsem.at[3 + j])
    of_ref[...] = (ah[zh] + rh[0] + rh[1] + rh[2]) / tokens
    arrived(attn_hbm, outsem.at[0])
    arrived(dq_hbm, outsem.at[1])
    sends.finish()
    for j in range(4):
        arrived(fr.at[j], gsem.at[10 + j])
    gf_ref[...] = (fr[0] + fr[1] + fr[2] + fr[3]) / tokens


def relay_in(rel, relsem, wide):
    group = pl.ds(0, 1) if wide == 0 else pl.ds(1, 3)
    for b in range(3):
        arrived(rel.at[b, group], relsem.at[b, wide])


def relay_out(sends, p, rel, kvs, rsem, g, up):
    for b in range(3):
        s = (3 - b) + (0 if b == 0 else p.core)
        rows = pl.ds(pl.multiple_of(s * TOK + p.x * QUARTER, QUARTER), QUARTER)
        sends.start(("relay", b), None, rel.at[b, g], kvs.at[p.core, g, rows, :],
                    rsem.at[p.core, s - 1, g], p.at(x=0, zh=up, core=0 if b == 0 else p.core), rel.at[0])


def fused(order, q, do, keys, values):
    vmem, hbm = pl.BlockSpec(memory_space=pltpu.VMEM), pl.BlockSpec(memory_space=pl.ANY)
    wide, all_lanes = KVH * HD, q.shape[1]
    V = pltpu.VMEM
    D = pltpu.SemaphoreType.DMA
    return pl.pallas_call(
        fused_kernel,
        out_shape=[
            jax.ShapeDtypeStruct((TOK, all_lanes), BF),
            jax.ShapeDtypeStruct((TOK, all_lanes), BF),
            jax.ShapeDtypeStruct((1, TOK, wide), BF),
            jax.ShapeDtypeStruct((1, TOK, wide), BF),
            jax.ShapeDtypeStruct((8, HD), F32),
            jax.ShapeDtypeStruct((2, 2 * HD), F32),
        ],
        in_specs=[pl.BlockSpec(memory_space=pltpu.SMEM)] + [hbm] * 4,
        out_specs=[hbm, hbm] + [vmem] * 4,
        scratch_shapes=[
            V((TOK, all_lanes), BF), V((TOK, all_lanes), BF), V((TOK, all_lanes), BF), V((TOK, all_lanes), BF),
            V((2, KVH, STEPS * TOK, HD), BF), V((2, KVH, STEPS * TOK, HD), BF),
            V((2, 16, HD, HD), BF), V((STEPS * TOK, TOK), F32),
            V((3, KVH, QUARTER, HD), BF), V((2, KVH, TOK, HD), BF), V((2, KVH, TOK, HD), BF),
            V((4, KVH, QUARTER, HD), BF), V((KVH, QUARTER, HD), BF), V((2, KVH, TOK, HD), BF), V((2, KVH, TOK, HD), BF),
            V((16, HD, HD), BF), V((4, 4, 128, HD), BF), V((4, 3, 128, HD), BF),
            V((4, 4, 32, HD), BF), V((4, 3, 32, HD), BF),
            V((4, 4, 8, HD), F32), V((3, 4, 8, HD), F32), V((4, 8, HD), F32), V((3, 8, HD), F32),
            V((4, TOK, 2 * HD), BF), V((3, TOK, 2 * HD), BF),
            V((2, 4, 32, 2 * HD), BF), V((4, 32, 2 * HD), BF), V((4, 32, 2 * HD), BF), V((3, 32, 2 * HD), BF),
            V((4, 8, 2 * HD), F32), V((3, 8, 2 * HD), F32), V((4, 2, 2 * HD), F32), V((4, 2, 2 * HD), F32),
            D((96,)), D((2, 4)), D((2,)), D((2,)), D((2, 3, 4)), D((3, 2)), D((2, 4)), D((4, 4)), D((2, 4)), D((2, 4)),
            D((4,)), D((4, 3)), D((4, 3)), D((6,)), D((14,)),
            pltpu.SemaphoreType.REGULAR, pltpu.SemaphoreType.REGULAR,
        ],
        compiler_params=pltpu.CompilerParams(
            collective_id=0, has_side_effects=True, vmem_limit_bytes=60 * 2**20),
    )(order, q, do, keys, values)


def local(queries, key_heads, value_heads, out_grad, block_order):
    outs = fused(block_order, queries[0], out_grad[0], key_heads[0], value_heads[0])
    attn, dq, dk, dv, out_factor, grad_factor = outs
    return attn[None], dq[None], dk, dv, out_factor, grad_factor


def solution(mesh):
    rows = P("dp", "ctx", None)
    return jax.shard_map(
        local,
        mesh=mesh,
        in_specs=(rows, rows, rows, rows, P()),
        out_specs=(rows, rows, rows, rows, P(("ctx", "dp"), None), P(("ctx", "dp"), None)),
        check_vma=False,
    )
```

time: 657 us -> 81.9 us (0.12)
  waiting for transfers between devices: 554 us -> 0 us
  Pallas kernels: 0 us -> 74.7 us
  starting transfers between devices: 43 us -> 0 us
  matrix products: 19.9 us -> 0 us
  between operations: 14.8 us -> 0.66 us
  local copies, waits for them, and re-layouts: 15.6 us -> 6.26 us
  other arithmetic: 8.05 us -> 0 us
    unnamed x2 -> x0, waiting for transfers between devices: 490 us -> none
    pallas_call x0 -> x1, Pallas kernels: none -> 74.7 us  [fused(): pl.pallas_call(fused_kernel, out_shape=[jax.ShapeDtypeStruct((TOK, all_la...]
    ppermute x14 -> x0, waiting for transfers between devices: 63.4 us -> none  [from_behind(): lax.ppermute(value, axis, [(i, (i + by) % size) for i in range(size)])]
    ppermute x14 -> x0, starting transfers between devices: 43 us -> none  [from_behind(): lax.ppermute(value, axis, [(i, (i + by) % size) for i in range(size)])]
    dot_general x26 -> x0, matrix products: 19.9 us -> none  [the longest x4 3.94 us: local(): jnp.einsum('tgjd,ugd->gjtu', grad_local, value_block, preferred_element_t...]
    unnamed x62 -> x16, local copies, waits for them, and re-layouts: 14.2 us -> 6.26 us
  transfers between devices with their start and end apart: 15 -> 0, of which waited for: 8 -> 0; matrix products, arithmetic and copies ran while one was open for 5% -> 0% of each run, Pallas kernels for 0% -> 0%
where the time goes in v2:
time: 81.9 us; the launch traced here: 81.6 us
  Pallas kernels  74.7 us (91%)
  local copies, waits for them, and re-layouts  6.26 us (8%)
    pallas_call x1, Pallas kernels, fused(): pl.pallas_call(fused_kernel, out_shape=[jax.ShapeDtypeStruct((TOK, all_la...  74.7 us
    unnamed x16, local copies, waits for them, and re-layouts  6.26 us

profile of v2, /device:TPU:1, one launch (start us, length us, event | category | flops | bytes accessed | tf_op | source)
XLA Modules:
  0.0 81.6 jit_solution(7680405249143270561)
XLA Ops:
  0.6 74.7 %shard_map.100 = (bf16[128,4096]{1,0:T(8,128)(2,1)}, bf16[128,4096]{1,0:T(8,128)(2,1)}, bf16[1,128,512]{2,1,0:T(8,128)(2,1)}, bf16[1,128,512]{2,1,0:T(8,128)(2,1)}, f32[8,128]{1,0:T(8,128)}, /*index=5*/f32[2,256]{1,0:T(2,128)}) custom-call(s32[64]{0:T(128)} %order_ref.1, bf16[128,4096]{1,0:T(8,128)(2,1)} %bitcast.6, bf16[128,4096]{1,0:T(8,128)(2,1)} %bitcast.7, ...), custom_call_target="tpu_custom_call" | custom-call | tf_op jit(solution)/shard_map/pallas_call | solution.py:493
  75.4 0.0 copy-start
  75.4 2.4 %copy.17 = bf16[1,128,4096]{2,1,0:T(8,128)(2,1)} copy(bf16[1,128,4096]{2,1,0:T(8,128)(2,1)} %bitcast.9) | data formatting | bytes 2097152
  77.8 0.0 copy-done
  77.8 0.0 copy-start.2
  77.8 1.0 %copy.18 = bf16[1,128,4096]{2,1,0:T(8,128)(2,1)} copy(bf16[1,128,4096]{2,1,0:T(8,128)(2,1)S(1)} %bitcast.8) | data formatting | bytes 2097152
  78.7 0.1 copy-done.2
  78.8 0.0 copy-start.1
  78.8 0.7 copy.19
  79.4 0.3 copy-done.1
  79.7 0.0 copy-start.3
  79.7 0.7 copy.20
  80.4 0.0 copy-done.3
  80.4 0.0 copy-start.4
  80.4 0.6 copy.21
  81.0 0.1 copy-done.4
  81.1 0.6 copy.22
Async XLA Ops:
  75.4 2.4 %copy-start = (bf16[128,4096]{1,0:T(8,128)(2,1)S(1)}, bf16[128,4096]{1,0:T(8,128)(2,1)}, u32[]{:S(2)}) copy-start(bf16[128,4096]{1,0:T(8,128)(2,1)} %get-tuple-element.13) | copy-start | bytes 3145732
  77.8 1.0 %copy-start.2 = (bf16[1,128,512]{2,1,0:T(8,128)(2,1)S(1)}, bf16[1,128,512]{2,1,0:T(8,128)(2,1)}, u32[]{:S(2)}) copy-start(bf16[1,128,512]{2,1,0:T(8,128)(2,1)} %get-tuple-element.26) | copy-start | bytes 393220
  78.8 1.0 %copy-start.1 = (bf16[1,128,512]{2,1,0:T(8,128)(2,1)S(1)}, bf16[1,128,512]{2,1,0:T(8,128)(2,1)}, u32[]{:S(2)}) copy-start(bf16[1,128,512]{2,1,0:T(8,128)(2,1)} %get-tuple-element.27) | copy-start | bytes 393220
  79.7 0.7 copy-start.3
  80.4 0.7 copy-start.4

commit v3 on v2

--- a/solution.py
+++ b/solution.py
@@ -117,9 +117,9 @@
     qv, dov, ov, dqv, kvs, dkv, gram, bias,
     rel, mate, snd, rel2, relsum, in1, in2,
     g0, ay, ry, ax, rx, az, rz, ah, rh,
-    zown, zin, cs, cr, xs, xr, ls, lr, fs, fr,
+    zown, order, cs, cr, ys, yr, xs, xr, zs, zr,
     ssem, qsem, outsem, ownsem, rsem, relsem, msem, rel2sem, in1sem, in2sem,
-    o0sem, oysem, oxsem, ozsem, gsem, ready2, ready3,
+    o0sem, oysem, oxsem, ozsem, gsem, zsem, ready2, ready3,
 ):
     p = Place()
     x, core, y, zl, zh = p.x, p.core, p.y, p.zl, p.zh
@@ -131,12 +131,12 @@
     sends = Sends(ssem)
 
     core0, core1 = core == 0, core == 1
-    x0, x_up, x0core0, x0core1 = x == 0, x >= 1, both(x == 0, core == 0), both(x == 0, core == 1)
+    x0, x_up, x0core0 = x == 0, x >= 1, both(x == 0, core == 0)
+    on0, on1 = both(x <= 2, core == 0), both(x <= 2, core == 1)
     tail_at = {0: x0core0, 1: both(x == 1, core == 0)}
     two_up = both(core == 0, x >= 2)
-    elsewhere = [y != g for g in range(KVH)]
     tall, thin, one_slot = mate.at[0], rel2.at[0], kvs.at[0, :, pl.ds(0, TOK), :]
-    one_ay, one_ax, one_z = ay.at[0], ax.at[0], zown.at[0]
+    one_ay, one_ax, one_gc, one_gy, one_gx = ay.at[0], ax.at[0], cr, ys.at[0], xs.at[0]
 
     signal(None, bar, p.at(zh=up))
     signal(None, bar, p.at(zh=down))
@@ -171,6 +171,10 @@
         for part in range(2):
             key_place = order_ref[2 * kc + part] * half + row
             bias[pl.ds(s * TOK + part * half, half), :] = jnp.where(key_place <= query_place, 0.0, NEG).astype(F32)
+    i = lax.broadcasted_iota(jnp.int32, (2 * HD, 2 * HD), 0)
+    q = lax.broadcasted_iota(jnp.int32, (2 * HD, 2 * HD), 1)
+    natural = ((q // 8) % 4) * 64 + (q // 128) * 32 + ((q // 2) % 4) * 8 + ((q // 32) % 4) * 2 + q % 2
+    order[...] = jnp.where(i == natural, 1.0, 0.0).astype(BF)
     pl.semaphore_wait(bar, 7 + 3 + 3 + 2 + 1 + core + 3)
 
     def slot(kind, s, g):
@@ -191,20 +195,18 @@
                 local_copy(both(owner, mine), piece, target, relsem.at[blk, wide])
     for g in range(KVH):
         for kind in range(2):
-            piece = slot(kind, 0, g)
-            s = 2 + kind - core
-            sends.start(("near", kind), x <= 2, piece, slot(kind, s, g), rsem.at[kind, s - 1, g],
-                        p.at(x=x + 1, core=kind), one_slot)
-            sends.start(("far", kind), both(x <= 1, core == 1), piece, slot(kind, 3, g), rsem.at[kind, 2, g],
-                        p.at(x=x + 2, core=0), one_slot)
-            sends.start(("own", kind), core == 0, piece, slot(kind, 1, g), rsem.at[kind, 0, g],
+            sends.start(("own", kind), core0, slot(kind, 0, g), slot(kind, 1, g), rsem.at[kind, 0, g],
                         p.at(core=1), one_slot)
-        if g == 0:
-            relay_in(rel, relsem, 0)
-            relay_out(sends, p, rel, kvs, rsem, 0, up)
+    relay_in(rel, relsem, 0)
+    relay_out(sends, p, rel, kvs, rsem, 0, up)
     relay_in(rel, relsem, 1)
     for g in range(1, KVH):
         relay_out(sends, p, rel, kvs, rsem, g, up)
+    for g in range(KVH):
+        for kind in range(2):
+            s = 2 + kind - core
+            sends.start(("near", kind), x <= 2, slot(kind, 0, g), slot(kind, s, g), rsem.at[kind, s - 1, g],
+                        p.at(x=x + 1, core=kind), one_slot)
     for side in (up, down):
         signal(None, ready2, p.at(zh=side))
 
@@ -217,10 +219,10 @@
             sends.start(("fv", s), core1, slot(1, s + 1, g), slot(1, s, g), rsem.at[1, s - 1, g],
                         p.at(core=0), one_slot)
             if s == 1:
-                sends.start(("f3k",), x0core0, slot(0, 1, g), slot(0, 3, g), rsem.at[0, 2, g],
-                            p.at(x=1, core=0), one_slot)
-                sends.start(("f3v",), x0core1, slot(1, 2, g), slot(1, 3, g), rsem.at[1, 2, g],
-                            p.at(x=1, core=0), one_slot)
+                sends.start(("f3k",), on0, slot(0, 1, g), slot(0, 3, g), rsem.at[0, 2, g],
+                            p.at(x=x + 1, core=0), one_slot)
+                sends.start(("f3v",), on1, slot(1, 2, g), slot(1, 3, g), rsem.at[1, 2, g],
+                            p.at(x=x + 1, core=0), one_slot)
 
     def slots_ready(g):
         @pl.when(core == 0)
@@ -338,8 +340,40 @@
                 outs[kind][0, :, lanes_of(g)] = (near + in2[kind, g].astype(F32)).astype(BF)
 
             zown[g, :, pl.ds(kind * HD, HD)] = outs[kind][0, :, lanes_of(g)]
-        at = ring(y, 7 - g)
-        sends.start(("z", g), elsewhere[g], zown.at[g], zin.at[at], gsem.at[at], p.at(y=g), one_z)
+
+    def factor1(g):
+        z = zown[g]
+        ordered = dot(z, order[...], 1, 0).astype(BF)
+        cs[g] = dot(ordered, z, 0, 0).reshape(2, 128, 2 * HD).astype(BF)
+        sends.start(("gc",), None, cs.at[g, other], cr.at[g], gsem.at[g, 0], p.at(core=other), one_gc)
+
+    def factor2(g):
+        arrived(cr.at[g], gsem.at[g, 0])
+        ys[g] = (cs[g, core].astype(F32) + cr[g].astype(F32)).reshape(4, 32, 2 * HD).astype(BF)
+        for j in (1, 2, 3):
+            sends.start(("gy", j), None, ys.at[g, ring(y, j)], yr.at[g, j - 1], gsem.at[g, j], p.at(y=ring(y, j)), one_gy)
+
+    def factor3(g):
+        total = ys[g, y].astype(F32)
+        for j in range(3):
+            arrived(yr.at[g, j], gsem.at[g, 1 + j])
+            total = total + yr[g, j].astype(F32)
+        xs[g] = total.reshape(4, 8, 2 * HD)
+        for j in (1, 2, 3):
+            sends.start(("gx", j), None, xs.at[g, ring(x, j)], xr.at[g, j - 1], gsem.at[g, 3 + j], p.at(x=ring(x, j)), one_gx)
+
+    def factor4(g):
+        total = xs[g, x]
+        for j in range(3):
+            arrived(xr.at[g, j], gsem.at[g, 4 + j])
+            total = total + xr[g, j]
+        mine = zh * 4 + zl
+        for j in range(4):
+            zs[g, j] = total[2 * j:2 * j + 2, :]
+            here = both(zh == g, zl == j)
+            sends.start(("gz", g, j), jnp.logical_not(here), zs.at[g, j], zr.at[mine], zsem.at[mine],
+                        p.at(zh=g, zl=j), zs.at[g, j])
+            local_copy(here, zs.at[g, j], zr.at[mine], zsem.at[mine])
 
     def out1(g):
         mine = pl.ds(4 * g, 4)
@@ -400,6 +434,7 @@
         @pl.when(g == 3)
         def _():
             home4(0)
+            factor1(0)
             out4(0)
         return 0
 
@@ -408,67 +443,52 @@
     home3(2)
     out2(3)
     out3(2)
+    pl.semaphore_wait(ready2, 2)
+    for j in (1, 2, 3):
+        signal(None, ready3, p.at(zl=ring(zl, j)))
     home4(1)
+    factor1(1)
+    home3(3)
+    factor2(0)
     out4(1)
-    home3(3)
     out3(3)
     home4(2)
+    factor1(2)
+    factor2(1)
+    factor3(0)
     out4(2)
-    pl.semaphore_wait(ready2, 2)
-    for j in (1, 2, 3):
-        signal(None, ready3, p.at(y=ring(y, j)))
     out4(3)
     for j in (1, 2, 3):
         sends.start(("oz", j), None, az.at[ring(zl, j)], rz.at[j - 1], ozsem.at[j - 1], p.at(zl=ring(zl, j)), rz.at[0])
     home4(3)
+    factor1(3)
+    factor2(2)
+    factor3(1)
+    pl.semaphore_wait(ready3, 3)
+    factor4(0)
+    factor2(3)
+    factor3(2)
+    factor4(1)
     for j in range(3):
         arrived(rz.at[j], ozsem.at[j])
     ah[...] = az[zl] + rz[0] + rz[1] + rz[2]
     for j in (1, 2, 3):
         sends.start(("oh", j), None, ah.at[ring(zh, j)], rh.at[j - 1], ozsem.at[2 + j], p.at(zh=ring(zh, j)), rh.at[0])
-
-    mine = zown[y]
-    total = dot(mine, mine, 0, 0)
-    for j in range(3):
-        arrived(zin.at[j], gsem.at[j])
-        z = zin[j]
-        total = total + dot(z, z, 0, 0)
-    total = total.reshape(4, 2, 32, 2 * HD)
-    for c2 in range(2):
-        cs[c2] = total[:, c2].astype(BF)
-    sends.start(("gc",), None, cs.at[other], cr, gsem.at[3], p.at(core=other), cr)
-    arrived(cr, gsem.at[3])
-    xs[...] = (cs[core].astype(F32) + cr[...].astype(F32)).astype(BF)
-    for j in (1, 2, 3):
-        sends.start(("gx", j), None, xs.at[ring(x, j)], xr.at[j - 1], gsem.at[3 + j], p.at(x=ring(x, j)), xr.at[0])
-    total = xs[x].astype(F32)
-    for j in range(3):
-        arrived(xr.at[j], gsem.at[4 + j])
-        total = total + xr[j].astype(F32)
-    ls[...] = total.reshape(4, 8, 2 * HD)
-    for j in (1, 2, 3):
-        sends.start(("gz", j), None, ls.at[ring(zl, j)], lr.at[j - 1], gsem.at[6 + j], p.at(zl=ring(zl, j)), lr.at[0])
-    pl.semaphore_wait(ready3, 3)
-    total = ls[zl]
-    for j in range(3):
-        arrived(lr.at[j], gsem.at[7 + j])
-        total = total + lr[j]
-    for j in range(4):
-        fs[j] = total[2 * j:2 * j + 2, :]
-    for j in range(4):
-        mine = both(y == j, zh == y)
-        sends.start(("gf", j), jnp.logical_not(mine), fs.at[j], fr.at[zh], gsem.at[10 + zh], p.at(y=j, zh=y), fr.at[0])
-        local_copy(mine, fs.at[j], fr.at[zh], gsem.at[10 + zh])
+    factor3(3)
+    factor4(2)
+    factor4(3)
+    arrived(attn_hbm, outsem.at[0])
+    arrived(dq_hbm, outsem.at[1])
     tokens = float(512 * TOK)
     for j in range(3):
         arrived(rh.at[j], ozsem.at[3 + j])
     of_ref[...] = (ah[zh] + rh[0] + rh[1] + rh[2]) / tokens
-    arrived(attn_hbm, outsem.at[0])
-    arrived(dq_hbm, outsem.at[1])
     sends.finish()
-    for j in range(4):
-        arrived(fr.at[j], gsem.at[10 + j])
-    gf_ref[...] = (fr[0] + fr[1] + fr[2] + fr[3]) / tokens
+    total = jnp.zeros((2, 2 * HD), F32)
+    for j in range(16):
+        arrived(zr.at[j], zsem.at[j])
+        total = total + zr[j]
+    gf_ref[...] = total / tokens
 
 
 def relay_in(rel, relsem, wide):
@@ -511,11 +531,13 @@
             V((16, HD, HD), BF), V((4, 4, 128, HD), BF), V((4, 3, 128, HD), BF),
             V((4, 4, 32, HD), BF), V((4, 3, 32, HD), BF),
             V((4, 4, 8, HD), F32), V((3, 4, 8, HD), F32), V((4, 8, HD), F32), V((3, 8, HD), F32),
-            V((4, TOK, 2 * HD), BF), V((3, TOK, 2 * HD), BF),
-            V((2, 4, 32, 2 * HD), BF), V((4, 32, 2 * HD), BF), V((4, 32, 2 * HD), BF), V((3, 32, 2 * HD), BF),
-            V((4, 8, 2 * HD), F32), V((3, 8, 2 * HD), F32), V((4, 2, 2 * HD), F32), V((4, 2, 2 * HD), F32),
+            V((4, TOK, 2 * HD), BF), V((2 * HD, 2 * HD), BF),
+            V((4, 2, 128, 2 * HD), BF), V((4, 128, 2 * HD), BF),
+            V((4, 4, 32, 2 * HD), BF), V((4, 3, 32, 2 * HD), BF),
+            V((4, 4, 8, 2 * HD), F32), V((4, 3, 8, 2 * HD), F32),
+            V((4, 4, 2, 2 * HD), F32), V((16, 2, 2 * HD), F32),
             D((96,)), D((2, 4)), D((2,)), D((2,)), D((2, 3, 4)), D((3, 2)), D((2, 4)), D((4, 4)), D((2, 4)), D((2, 4)),
-            D((4,)), D((4, 3)), D((4, 3)), D((6,)), D((14,)),
+            D((4,)), D((4, 3)), D((4, 3)), D((6,)), D((4, 7)), D((16,)),
             pltpu.SemaphoreType.REGULAR, pltpu.SemaphoreType.REGULAR,
         ],
         compiler_params=pltpu.CompilerParams(
@@ -523,9 +545,31 @@
     )(order, q, do, keys, values)
 
 
+def handover_kernel(*refs):
+    count = len(refs) // 2
+    for i in range(count):
+        refs[count + i][...] = refs[i][...]
+
+
+def handover(attn, dq, dk, dv, out_factor, grad_factor):
+    arrays = (attn, dq, dk, dv, out_factor, grad_factor)
+    steps = 4
+    big = pl.BlockSpec((TOK, attn.shape[1] // steps), lambda i: (0, i))
+    small = pl.BlockSpec((1, TOK, dk.shape[2] // steps), lambda i: (0, 0, i))
+    whole = [pl.BlockSpec(a.shape, lambda i: (0, 0)) for a in (out_factor, grad_factor)]
+    specs = [big, big, small, small] + whole
+    return pl.pallas_call(
+        handover_kernel,
+        grid=(steps,),
+        out_shape=[jax.ShapeDtypeStruct(a.shape, a.dtype) for a in arrays],
+        in_specs=specs,
+        out_specs=specs,
+    )(*arrays)
+
+
 def local(queries, key_heads, value_heads, out_grad, block_order):
     outs = fused(block_order, queries[0], out_grad[0], key_heads[0], value_heads[0])
-    attn, dq, dk, dv, out_factor, grad_factor = outs
+    attn, dq, dk, dv, out_factor, grad_factor = handover(*outs)
     return attn[None], dq[None], dk, dv, out_factor, grad_factor
 
 

time: 81.9 us -> 72.8 us (0.89)
  the two profiles are of different devices: /device:TPU:1 before, /device:TPU:32 now
where the time goes in v3:
time: 72.8 us; the launch traced here: 72.6 us
  Pallas kernels  71.9 us (99%)
    pallas_call x1, Pallas kernels, fused(): pl.pallas_call(fused_kernel, out_shape=[jax.ShapeDtypeStruct((TOK, all_la...  68.1 us
    pallas_call x1, Pallas kernels, handover(): pl.pallas_call(handover_kernel, grid=(steps,), out_shape=[jax.ShapeDtypeS...  3.81 us

profile of v3, /device:TPU:32, one launch (start us, length us, event | category | flops | bytes accessed | tf_op | source)
XLA Modules:
  0.0 72.6 jit_solution(13415325567461456720)
XLA Ops:
  0.6 68.1 %shard_map.100 = (bf16[128,4096]{1,0:T(8,128)(2,1)}, bf16[128,4096]{1,0:T(8,128)(2,1)}, bf16[1,128,512]{2,1,0:T(8,128)(2,1)}, bf16[1,128,512]{2,1,0:T(8,128)(2,1)}, f32[8,128]{1,0:T(8,128)}, /*index=5*/f32[2,256]{1,0:T(2,128)}) custom-call(s32[64]{0:T(128)} %order_ref.1, bf16[128,4096]{1,0:T(8,128)(2,1)} %bitcast.6, bf16[128,4096]{1,0:T(8,128)(2,1)} %bitcast.7, ...), custom_call_target="tpu_custom_call" | custom-call | tf_op jit(solution)/shard_map/pallas_call | solution.py:513
  68.7 3.8 %shard_map.101 = (bf16[128,4096]{1,0:T(8,128)(2,1)}, bf16[128,4096]{1,0:T(8,128)(2,1)}, bf16[1,128,512]{2,1,0:T(8,128)(2,1)}, bf16[1,128,512]{2,1,0:T(8,128)(2,1)}, f32[8,128]{1,0:T(8,128)}, /*index=5*/f32[2,256]{1,0:T(2,128)}) custom-call(bf16[128,4096]{1,0:T(8,128)(2,1)} %get-tuple-element.18.refs_0_, bf16[128,4096]{1,0:T(8,128)(2,1)} %get-tuple-element.19.refs_1_, ...), custom_call_target="tpu_custom_call" | custom-call | tf_op jit(solution)/shard_map/pallas_call | solution.py:561

commit v4 on v3

--- a/solution.py
+++ b/solution.py
@@ -48,11 +48,11 @@
 
 class Sends:
     def __init__(self, sems):
-        self.sems, self.keys = sems, {}
+        self.sems, self.keys, self.always = sems, {}, {}
 
     def start(self, key, cond, src, dst, recv_sem, device, whole):
         if key not in self.keys:
-            self.keys[key] = (len(self.keys), cond, whole)
+            self.keys[key] = (len(self.keys), self.always.get(key, cond), whole)
         copy = pltpu.make_async_remote_copy(
             src_ref=src, dst_ref=dst, send_sem=self.sems.at[self.keys[key][0]], recv_sem=recv_sem,
             device_id=device, device_id_type=MESH,
@@ -119,7 +119,7 @@
     g0, ay, ry, ax, rx, az, rz, ah, rh,
     zown, order, cs, cr, ys, yr, xs, xr, zs, zr,
     ssem, qsem, outsem, ownsem, rsem, relsem, msem, rel2sem, in1sem, in2sem,
-    o0sem, oysem, oxsem, ozsem, gsem, zsem, ready2, ready3,
+    o0sem, oysem, oxsem, ozsem, gsem, zsem, ready1, ready2, ready3,
 ):
     p = Place()
     x, core, y, zl, zh = p.x, p.core, p.y, p.zl, p.zh
@@ -129,23 +129,19 @@
     blk = 2 * (x - 2) + core - 1
     bar = pltpu.get_barrier_semaphore()
     sends = Sends(ssem)
+    sends.always = {"spread": owner, "gz": None}
 
     core0, core1 = core == 0, core == 1
     x0, x_up, x0core0 = x == 0, x >= 1, both(x == 0, core == 0)
     on0, on1 = both(x <= 2, core == 0), both(x <= 2, core == 1)
     tail_at = {0: x0core0, 1: both(x == 1, core == 0)}
     two_up = both(core == 0, x >= 2)
-    tall, thin, one_slot = mate.at[0], rel2.at[0], kvs.at[0, :, pl.ds(0, TOK), :]
-    one_ay, one_ax, one_gc, one_gy, one_gx = ay.at[0], ax.at[0], cr, ys.at[0], xs.at[0]
+    blocks = {n: gram.at[0, pl.ds(0, n)] for n in (3, 4, 6, 7, 8, 12, 16)}
+    blocks[24] = kvs.at[:, pl.ds(0, 3)]
+    all_z = zr.at[pl.ds(0, 15)]
 
     signal(None, bar, p.at(zh=up))
     signal(None, bar, p.at(zh=down))
-    for j in range(4):
-        signal(x == 0, bar, p.at(x=j, zh=down))
-        signal(both(x == 0, core == 0), bar, p.at(x=j, core=1, zh=down))
-        for t in range(2):
-            signal(x == 3, bar, p.at(x=j, core=t, zh=up))
-            signal(both(x == 2, core == 1), bar, p.at(x=j, core=t, zh=up))
     for j in (1, 2, 3):
         signal(None, bar, p.at(zl=ring(zl, j)))
         signal(None, bar, p.at(y=ring(y, j)))
@@ -175,7 +171,7 @@
     q = lax.broadcasted_iota(jnp.int32, (2 * HD, 2 * HD), 1)
     natural = ((q // 8) % 4) * 64 + (q // 128) * 32 + ((q // 2) % 4) * 8 + ((q // 32) % 4) * 2 + q % 2
     order[...] = jnp.where(i == natural, 1.0, 0.0).astype(BF)
-    pl.semaphore_wait(bar, 7 + 3 + 3 + 2 + 1 + core + 3)
+    pl.semaphore_wait(bar, 7 + 3 + 3 + 2)
 
     def slot(kind, s, g):
         return kvs.at[kind, g, pl.ds(s * TOK, TOK), :]
@@ -190,23 +186,32 @@
                 mine = both(x == j, core == t)
                 piece = kvs.at[t, group, pl.ds(j * QUARTER, QUARTER), :]
                 target = rel.at[blk, group]
-                sends.start(("spread", j, t), both(owner, jnp.logical_not(mine)), piece, target,
-                            relsem.at[blk, wide], p.at(x=j, core=t), rel.at[0])
+                sends.start("spread", both(owner, jnp.logical_not(mine)), piece, target,
+                            relsem.at[blk, wide], p.at(x=j, core=t), blocks[7])
                 local_copy(both(owner, mine), piece, target, relsem.at[blk, wide])
+    for j in range(4):
+        for t in range(2):
+            signal(jnp.logical_not(both(x == j, core == t)), ready1, p.at(x=j, core=t))
     for g in range(KVH):
         for kind in range(2):
-            sends.start(("own", kind), core0, slot(kind, 0, g), slot(kind, 1, g), rsem.at[kind, 0, g],
-                        p.at(core=1), one_slot)
+            sends.start("core0", core0, slot(kind, 0, g), slot(kind, 1, g), rsem.at[kind, 0, g],
+                        p.at(core=1), blocks[24])
+    for g in range(2):
+        for kind in range(2):
+            s = 2 + kind - core
+            sends.start("near", x <= 2, slot(kind, 0, g), slot(kind, s, g), rsem.at[kind, s - 1, g],
+                        p.at(x=x + 1, core=kind), blocks[8])
+    pl.semaphore_wait(ready1, 7)
     relay_in(rel, relsem, 0)
-    relay_out(sends, p, rel, kvs, rsem, 0, up)
+    relay_out(sends, p, rel, kvs, rsem, 0, up, blocks[3])
     relay_in(rel, relsem, 1)
     for g in range(1, KVH):
-        relay_out(sends, p, rel, kvs, rsem, g, up)
-    for g in range(KVH):
+        relay_out(sends, p, rel, kvs, rsem, g, up, blocks[3])
+    for g in range(2, KVH):
         for kind in range(2):
             s = 2 + kind - core
-            sends.start(("near", kind), x <= 2, slot(kind, 0, g), slot(kind, s, g), rsem.at[kind, s - 1, g],
-                        p.at(x=x + 1, core=kind), one_slot)
+            sends.start("near", x <= 2, slot(kind, 0, g), slot(kind, s, g), rsem.at[kind, s - 1, g],
+                        p.at(x=x + 1, core=kind), blocks[8])
     for side in (up, down):
         signal(None, ready2, p.at(zh=side))
 
@@ -214,15 +219,15 @@
         for s in (1, 2):
             pl.when(core == 0)(lambda: arrived(slot(0, s, g), rsem.at[0, s - 1, g]))
             pl.when(core == 1)(lambda: arrived(slot(1, s + 1, g), rsem.at[1, s, g]))
-            sends.start(("fk", s), core0, slot(0, s, g), slot(0, s + 1, g), rsem.at[0, s, g],
-                        p.at(core=1), one_slot)
-            sends.start(("fv", s), core1, slot(1, s + 1, g), slot(1, s, g), rsem.at[1, s - 1, g],
-                        p.at(core=0), one_slot)
+            sends.start("core0", core0, slot(0, s, g), slot(0, s + 1, g), rsem.at[0, s, g],
+                        p.at(core=1), blocks[24])
+            sends.start("core1", core1, slot(1, s + 1, g), slot(1, s, g), rsem.at[1, s - 1, g],
+                        p.at(core=0), blocks[24])
             if s == 1:
-                sends.start(("f3k",), on0, slot(0, 1, g), slot(0, 3, g), rsem.at[0, 2, g],
-                            p.at(x=x + 1, core=0), one_slot)
-                sends.start(("f3v",), on1, slot(1, 2, g), slot(1, 3, g), rsem.at[1, 2, g],
-                            p.at(x=x + 1, core=0), one_slot)
+                sends.start("f3k", on0, slot(0, 1, g), slot(0, 3, g), rsem.at[0, 2, g],
+                            p.at(x=x + 1, core=0), blocks[4])
+                sends.start("f3v", on1, slot(1, 2, g), slot(1, 3, g), rsem.at[1, 2, g],
+                            p.at(x=x + 1, core=0), blocks[4])
 
     def slots_ready(g):
         @pl.when(core == 0)
@@ -261,6 +266,7 @@
         ds = jnp.concatenate(dscores, axis=1)
         dkv[1, g] = dot(pb, do_all, 1, 0).astype(BF)
         dkv[0, g] = (dot(ds, q_all, 1, 0) * SCALE).astype(BF)
+        home1(g)
         ot = dot(jnp.transpose(values), pb, 1, 0).astype(BF)
         dqt = (dot(jnp.transpose(keys), ds, 1, 0) * SCALE).astype(BF)
         for h in range(8):
@@ -277,8 +283,8 @@
 
     def home1(g):
         for i in range(2):
-            sends.start(("mv", i), core0, part(1, 1 + i, g), mate.at[i, g], msem.at[i, g], p.at(core=1), tall)
-            sends.start(("mk", i), core1, part(0, 2 + i, g), mate.at[i, g], msem.at[i, g], p.at(core=0), tall)
+            sends.start("core0", core0, part(1, 1 + i, g), mate.at[i, g], msem.at[i, g], p.at(core=1), blocks[24])
+            sends.start("core1", core1, part(0, 2 + i, g), mate.at[i, g], msem.at[i, g], p.at(core=0), blocks[24])
         for kind in range(2):
             for j in range(4):
                 piece = dkv.at[kind, g, pl.ds(3 * TOK + j * QUARTER, QUARTER), :]
@@ -287,11 +293,11 @@
                     if kind == 0 and j == sx:
                         local_copy(here, piece, rel2.at[b, g], rel2sem.at[b, g])
                     else:
-                        sends.start(("r3", kind, j, b), here, piece, rel2.at[b, g], rel2sem.at[b, g],
-                                    p.at(x=j, core=kind), thin)
-            sends.start(("m1", kind), core1, part(kind, 1, g), in2.at[kind, g], in2sem.at[kind, g], p.at(core=0), tall)
-            sends.start(("m3", kind), two_up, part(kind, 3, g), in2.at[kind, g],
-                        in2sem.at[kind, g], p.at(x=x - 2, core=1), tall)
+                        sends.start(("tail", sx), here, piece, rel2.at[b, g], rel2sem.at[b, g],
+                                    p.at(x=j, core=kind), blocks[7])
+            sends.start("core1", core1, part(kind, 1, g), in2.at[kind, g], in2sem.at[kind, g], p.at(core=0), blocks[24])
+            sends.start("m3", two_up, part(kind, 3, g), in2.at[kind, g],
+                        in2sem.at[kind, g], p.at(x=x - 2, core=1), blocks[8])
 
     def home2(g):
         for i in range(2):
@@ -299,28 +305,28 @@
             rows = pl.ds(pl.multiple_of((1 + i + core) * TOK, TOK), TOK)
             mine = dkv[core, g, rows, :]
             snd[i, g] = (mine.astype(F32) + mate[i, g].astype(F32)).astype(BF)
-            sends.start(("n", i), x_up, snd.at[i, g], in1.at[core, g], in1sem.at[core, g],
-                        p.at(x=x - 1, core=1 - i), tall)
+            sends.start("n", x_up, snd.at[i, g], in1.at[core, g], in1sem.at[core, g],
+                        p.at(x=x - 1, core=1 - i), blocks[8])
             for j in range(4):
                 piece = snd.at[i, g, pl.ds(j * QUARTER, QUARTER), :]
                 if j == 0:
                     local_copy(x0, piece, rel2.at[i, g], rel2sem.at[i, g])
                 else:
-                    sends.start(("r", i, j), x0, piece, rel2.at[i, g], rel2sem.at[i, g], p.at(x=j), thin)
+                    sends.start("r", x0, piece, rel2.at[i, g], rel2sem.at[i, g], p.at(x=j), blocks[6])
 
     def home3(g):
         def there(ref):
             return ref.at[core, g, rows_of(x), :]
 
         arrived(rel2.at[2, g], rel2sem.at[2, g])
-        sends.start(("h2",), None, rel2.at[2, g], there(in2), in2sem.at[core, g], p.at(x=2, core=1, zh=down), thin)
+        sends.start("home", None, rel2.at[2, g], there(in2), in2sem.at[core, g], p.at(x=2, core=1, zh=down), blocks[3])
         arrived(rel2.at[1, g], rel2sem.at[1, g])
-        sends.start(("h1",), None, rel2.at[1, g], there(in1), in1sem.at[core, g], p.at(x=3, core=0, zh=down), thin)
+        sends.start("home", None, rel2.at[1, g], there(in1), in1sem.at[core, g], p.at(x=3, core=0, zh=down), blocks[3])
         arrived(rel2.at[0, g], rel2sem.at[0, g])
         arrived(rel2.at[3, g], rel2sem.at[3, g])
         relsum[g] = (
             rel2[0, g].astype(F32) + rel2[3, g].astype(F32)).astype(BF)
-        sends.start(("h0",), None, relsum.at[g], there(in1), in1sem.at[core, g], p.at(x=3, core=1, zh=down), thin)
+        sends.start("home", None, relsum.at[g], there(in1), in1sem.at[core, g], p.at(x=3, core=1, zh=down), blocks[3])
 
     last = both(x == 3, core == 1)
     outs = (dk_ref, dv_ref)
@@ -345,39 +351,39 @@
         z = zown[g]
         ordered = dot(z, order[...], 1, 0).astype(BF)
         cs[g] = dot(ordered, z, 0, 0).reshape(2, 128, 2 * HD).astype(BF)
-        sends.start(("gc",), None, cs.at[g, other], cr.at[g], gsem.at[g, 0], p.at(core=other), one_gc)
+        sends.start("gc", None, cs.at[g, other], cr.at[g], gsem.at[g, 0], p.at(core=other), blocks[8])
 
     def factor2(g):
         arrived(cr.at[g], gsem.at[g, 0])
         ys[g] = (cs[g, core].astype(F32) + cr[g].astype(F32)).reshape(4, 32, 2 * HD).astype(BF)
         for j in (1, 2, 3):
-            sends.start(("gy", j), None, ys.at[g, ring(y, j)], yr.at[g, j - 1], gsem.at[g, j], p.at(y=ring(y, j)), one_gy)
+            sends.start("gy", None, ys.at[g, ring(y, j)], yr.at[g, j - 1], gsem.at[g, 1], p.at(y=ring(y, j)), blocks[6])
 
     def factor3(g):
+        arrived(yr.at[g], gsem.at[g, 1])
         total = ys[g, y].astype(F32)
         for j in range(3):
-            arrived(yr.at[g, j], gsem.at[g, 1 + j])
             total = total + yr[g, j].astype(F32)
         xs[g] = total.reshape(4, 8, 2 * HD)
         for j in (1, 2, 3):
-            sends.start(("gx", j), None, xs.at[g, ring(x, j)], xr.at[g, j - 1], gsem.at[g, 3 + j], p.at(x=ring(x, j)), one_gx)
+            sends.start("gx", None, xs.at[g, ring(x, j)], xr.at[g, j - 1], gsem.at[g, 2], p.at(x=ring(x, j)), blocks[3])
 
     def factor4(g):
+        arrived(xr.at[g], gsem.at[g, 2])
         total = xs[g, x]
         for j in range(3):
-            arrived(xr.at[g, j], gsem.at[g, 4 + j])
             total = total + xr[g, j]
         mine = zh * 4 + zl
         for j in range(4):
             zs[g, j] = total[2 * j:2 * j + 2, :]
             here = both(zh == g, zl == j)
-            sends.start(("gz", g, j), jnp.logical_not(here), zs.at[g, j], zr.at[mine], zsem.at[mine],
-                        p.at(zh=g, zl=j), zs.at[g, j])
-            local_copy(here, zs.at[g, j], zr.at[mine], zsem.at[mine])
+            sends.start("gz", jnp.logical_not(here), zs.at[g, j], zr.at[mine], zsem.at[0],
+                        p.at(zh=g, zl=j), all_z)
+            local_copy(here, zs.at[g, j], zr.at[mine], zsem.at[0])
 
     def out1(g):
         mine = pl.ds(4 * g, 4)
-        sends.start(("oc",), None, gram.at[other, mine], g0.at[mine], o0sem.at[g], p.at(core=other), g0)
+        sends.start("oc", None, gram.at[other, mine], g0.at[mine], o0sem.at[g], p.at(core=other), blocks[16])
 
     def out2(g):
         arrived(g0.at[pl.ds(4 * g, 4)], o0sem.at[g])
@@ -387,21 +393,19 @@
             for j in range(4):
                 ay[g, j, pl.ds(h * 32, 32), :] = split[:, j].reshape(32, HD).astype(BF)
         for j in (1, 2, 3):
-            sends.start(("oy", j), None, ay.at[g, ring(y, j)], ry.at[g, j - 1], oysem.at[g, j - 1], p.at(y=ring(y, j)), one_ay)
+            sends.start("oy", None, ay.at[g, ring(y, j)], ry.at[g, j - 1], oysem.at[g], p.at(y=ring(y, j)), blocks[12])
 
     def out3(g):
-        for j in range(3):
-            arrived(ry.at[g, j], oysem.at[g, j])
+        arrived(ry.at[g], oysem.at[g])
         total = ay[g, y].astype(F32)
         for j in range(3):
             total = total + ry[g, j].astype(F32)
         ax[g] = total.reshape(4, 32, HD).astype(BF)
         for j in (1, 2, 3):
-            sends.start(("ox", j), None, ax.at[g, ring(x, j)], rx.at[g, j - 1], oxsem.at[g, j - 1], p.at(x=ring(x, j)), one_ax)
+            sends.start("ox", None, ax.at[g, ring(x, j)], rx.at[g, j - 1], oxsem.at[g], p.at(x=ring(x, j)), blocks[3])
 
     def out4(g):
-        for j in range(3):
-            arrived(rx.at[g, j], oxsem.at[g, j])
+        arrived(rx.at[g], oxsem.at[g])
         total = ax[g, x].astype(F32)
         for j in range(3):
             total = total + rx[g, j].astype(F32)
@@ -418,7 +422,6 @@
         arrived(qv.at[:, heads], qsem.at[0, g])
         arrived(dov.at[:, heads], qsem.at[1, g])
         compute(g)
-        home1(g)
         out1(g)
 
         @pl.when(g >= 1)
@@ -459,7 +462,7 @@
     out4(2)
     out4(3)
     for j in (1, 2, 3):
-        sends.start(("oz", j), None, az.at[ring(zl, j)], rz.at[j - 1], ozsem.at[j - 1], p.at(zl=ring(zl, j)), rz.at[0])
+        sends.start("oz", None, az.at[ring(zl, j)], rz.at[j - 1], ozsem.at[0], p.at(zl=ring(zl, j)), rz)
     home4(3)
     factor1(3)
     factor2(2)
@@ -469,24 +472,22 @@
     factor2(3)
     factor3(2)
     factor4(1)
-    for j in range(3):
-        arrived(rz.at[j], ozsem.at[j])
+    arrived(rz, ozsem.at[0])
     ah[...] = az[zl] + rz[0] + rz[1] + rz[2]
     for j in (1, 2, 3):
-        sends.start(("oh", j), None, ah.at[ring(zh, j)], rh.at[j - 1], ozsem.at[2 + j], p.at(zh=ring(zh, j)), rh.at[0])
+        sends.start("oh", None, ah.at[ring(zh, j)], rh.at[j - 1], ozsem.at[1], p.at(zh=ring(zh, j)), rh)
     factor3(3)
     factor4(2)
     factor4(3)
     arrived(attn_hbm, outsem.at[0])
     arrived(dq_hbm, outsem.at[1])
     tokens = float(512 * TOK)
-    for j in range(3):
-        arrived(rh.at[j], ozsem.at[3 + j])
+    arrived(rh, ozsem.at[1])
     of_ref[...] = (ah[zh] + rh[0] + rh[1] + rh[2]) / tokens
     sends.finish()
     total = jnp.zeros((2, 2 * HD), F32)
+    arrived(zr, zsem.at[0])
     for j in range(16):
-        arrived(zr.at[j], zsem.at[j])
         total = total + zr[j]
     gf_ref[...] = total / tokens
 
@@ -497,12 +498,12 @@
         arrived(rel.at[b, group], relsem.at[b, wide])
 
 
-def relay_out(sends, p, rel, kvs, rsem, g, up):
+def relay_out(sends, p, rel, kvs, rsem, g, up, relayed):
     for b in range(3):
         s = (3 - b) + (0 if b == 0 else p.core)
         rows = pl.ds(pl.multiple_of(s * TOK + p.x * QUARTER, QUARTER), QUARTER)
-        sends.start(("relay", b), None, rel.at[b, g], kvs.at[p.core, g, rows, :],
-                    rsem.at[p.core, s - 1, g], p.at(x=0, zh=up, core=0 if b == 0 else p.core), rel.at[0])
+        sends.start("relay", None, rel.at[b, g], kvs.at[p.core, g, rows, :],
+                    rsem.at[p.core, s - 1, g], p.at(x=0, zh=up, core=0 if b == 0 else p.core), relayed)
 
 
 def fused(order, q, do, keys, values):
@@ -536,9 +537,9 @@
             V((4, 4, 32, 2 * HD), BF), V((4, 3, 32, 2 * HD), BF),
             V((4, 4, 8, 2 * HD), F32), V((4, 3, 8, 2 * HD), F32),
             V((4, 4, 2, 2 * HD), F32), V((16, 2, 2 * HD), F32),
-            D((96,)), D((2, 4)), D((2,)), D((2,)), D((2, 3, 4)), D((3, 2)), D((2, 4)), D((4, 4)), D((2, 4)), D((2, 4)),
-            D((4,)), D((4, 3)), D((4, 3)), D((6,)), D((4, 7)), D((16,)),
-            pltpu.SemaphoreType.REGULAR, pltpu.SemaphoreType.REGULAR,
+            D((24,)), D((2, 4)), D((2,)), D((2,)), D((2, 3, 4)), D((3, 2)), D((2, 4)), D((4, 4)), D((2, 4)), D((2, 4)),
+            D((4,)), D((4,)), D((4,)), D((2,)), D((4, 3)), D((1,)),
+            pltpu.SemaphoreType.REGULAR, pltpu.SemaphoreType.REGULAR, pltpu.SemaphoreType.REGULAR,
         ],
         compiler_params=pltpu.CompilerParams(
             collective_id=0, has_side_effects=True, vmem_limit_bytes=60 * 2**20),
@@ -553,9 +554,9 @@
 
 def handover(attn, dq, dk, dv, out_factor, grad_factor):
     arrays = (attn, dq, dk, dv, out_factor, grad_factor)
-    steps = 4
-    big = pl.BlockSpec((TOK, attn.shape[1] // steps), lambda i: (0, i))
-    small = pl.BlockSpec((1, TOK, dk.shape[2] // steps), lambda i: (0, 0, i))
+    steps = 2
+    big = pl.BlockSpec((TOK // steps, attn.shape[1]), lambda i: (i, 0))
+    small = pl.BlockSpec((1, TOK // steps, dk.shape[2]), lambda i: (0, i, 0))
     whole = [pl.BlockSpec(a.shape, lambda i: (0, 0)) for a in (out_factor, grad_factor)]
     specs = [big, big, small, small] + whole
     return pl.pallas_call(

time: 72.8 us -> 69.4 us (0.953)
  the two profiles are of different devices: /device:TPU:32 before, /device:TPU:1 now
where the time goes in v4:
time: 69.4 us; the launch traced here: 68.9 us
  Pallas kernels  68.3 us (98%)
    pallas_call x1, Pallas kernels, fused(): pl.pallas_call(fused_kernel, out_shape=[jax.ShapeDtypeStruct((TOK, all_la...  65.4 us
    pallas_call x1, Pallas kernels, handover(): pl.pallas_call(handover_kernel, grid=(steps,), out_shape=[jax.ShapeDtypeS...  2.84 us

profile of v4, /device:TPU:1, one launch (start us, length us, event | category | flops | bytes accessed | tf_op | source)
XLA Modules:
  0.0 68.9 jit_solution(14596983376901121495)
XLA Ops:
  0.6 65.4 %shard_map.100 = (bf16[128,4096]{1,0:T(8,128)(2,1)}, bf16[128,4096]{1,0:T(8,128)(2,1)}, bf16[1,128,512]{2,1,0:T(8,128)(2,1)}, bf16[1,128,512]{2,1,0:T(8,128)(2,1)}, f32[8,128]{1,0:T(8,128)}, /*index=5*/f32[2,256]{1,0:T(2,128)}) custom-call(s32[64]{0:T(128)} %order_ref.1, bf16[128,4096]{1,0:T(8,128)(2,1)} %bitcast.6, bf16[128,4096]{1,0:T(8,128)(2,1)} %bitcast.7, ...), custom_call_target="tpu_custom_call" | custom-call | tf_op jit(solution)/shard_map/pallas_call | solution.py:514
  66.1 2.8 %shard_map.101 = (bf16[128,4096]{1,0:T(8,128)(2,1)}, bf16[128,4096]{1,0:T(8,128)(2,1)}, bf16[1,128,512]{2,1,0:T(8,128)(2,1)}, bf16[1,128,512]{2,1,0:T(8,128)(2,1)}, f32[8,128]{1,0:T(8,128)}, /*index=5*/f32[2,256]{1,0:T(2,128)}) custom-call(bf16[128,4096]{1,0:T(8,128)(2,1)} %get-tuple-element.18.refs_0_, bf16[128,4096]{1,0:T(8,128)(2,1)} %get-tuple-element.19.refs_1_, ...), custom_call_target="tpu_custom_call" | custom-call | tf_op jit(solution)/shard_map/pallas_call | solution.py:562

commit v5 on v4

--- a/solution.py
+++ b/solution.py
@@ -112,13 +112,13 @@
 
 
 def fused_kernel(
-    order_ref, q_hbm, do_hbm, k_hbm, v_hbm,
+    order_hbm, q_hbm, do_hbm, k_hbm, v_hbm,
     attn_hbm, dq_hbm, dk_ref, dv_ref, of_ref, gf_ref,
-    qv, dov, ov, dqv, kvs, dkv, gram, bias,
+    order_ref, qv, dov, ov, dqv, kvs, dkv, gram, bias,
     rel, mate, snd, rel2, relsum, in1, in2,
     g0, ay, ry, ax, rx, az, rz, ah, rh,
     zown, order, cs, cr, ys, yr, xs, xr, zs, zr,
-    ssem, qsem, outsem, ownsem, rsem, relsem, msem, rel2sem, in1sem, in2sem,
+    ssem, qsem, ordersem, outsem, ownsem, rsem, relsem, msem, rel2sem, in1sem, in2sem,
     o0sem, oysem, oxsem, ozsem, gsem, zsem, ready1, ready2, ready3,
 ):
     p = Place()
@@ -140,6 +140,7 @@
     blocks[24] = kvs.at[:, pl.ds(0, 3)]
     all_z = zr.at[pl.ds(0, 15)]
 
+    local_copy(None, order_hbm, order_ref, ordersem.at[0])
     signal(None, bar, p.at(zh=up))
     signal(None, bar, p.at(zh=down))
     for j in (1, 2, 3):
@@ -157,6 +158,7 @@
             for kind in range(2):
                 for i in range(KVH):
                     local_copy(None, own[kind].at[:, lanes_of(i)], kvs.at[kind, i, pl.ds(0, TOK), :], ownsem.at[kind])
+    arrived(order_ref, ordersem.at[0])
     half = TOK // 2
     c = lax.axis_index("ctx")
     row = lax.broadcasted_iota(jnp.int32, (half, TOK), 0)
@@ -521,9 +523,10 @@
             jax.ShapeDtypeStruct((8, HD), F32),
             jax.ShapeDtypeStruct((2, 2 * HD), F32),
         ],
-        in_specs=[pl.BlockSpec(memory_space=pltpu.SMEM)] + [hbm] * 4,
+        in_specs=[hbm] * 5,
         out_specs=[hbm, hbm] + [vmem] * 4,
         scratch_shapes=[
+            pltpu.SMEM(order.shape, order.dtype),
             V((TOK, all_lanes), BF), V((TOK, all_lanes), BF), V((TOK, all_lanes), BF), V((TOK, all_lanes), BF),
             V((2, KVH, STEPS * TOK, HD), BF), V((2, KVH, STEPS * TOK, HD), BF),
             V((2, 16, HD, HD), BF), V((STEPS * TOK, TOK), F32),
@@ -537,7 +540,7 @@
             V((4, 4, 32, 2 * HD), BF), V((4, 3, 32, 2 * HD), BF),
             V((4, 4, 8, 2 * HD), F32), V((4, 3, 8, 2 * HD), F32),
             V((4, 4, 2, 2 * HD), F32), V((16, 2, 2 * HD), F32),
-            D((24,)), D((2, 4)), D((2,)), D((2,)), D((2, 3, 4)), D((3, 2)), D((2, 4)), D((4, 4)), D((2, 4)), D((2, 4)),
+            D((24,)), D((2, 4)), D((1,)), D((2,)), D((2,)), D((2, 3, 4)), D((3, 2)), D((2, 4)), D((4, 4)), D((2, 4)), D((2, 4)),
             D((4,)), D((4,)), D((4,)), D((2,)), D((4, 3)), D((1,)),
             pltpu.SemaphoreType.REGULAR, pltpu.SemaphoreType.REGULAR, pltpu.SemaphoreType.REGULAR,
         ],

time: 69.4 us -> 68.8 us (level)
  Pallas kernels: 68.3 us -> 67.6 us
where the time goes in v5:
time: 68.8 us; the launch traced here: 68.3 us
  Pallas kernels  67.6 us (98%)
    pallas_call x1, Pallas kernels, fused(): pl.pallas_call(fused_kernel, out_shape=[jax.ShapeDtypeStruct((TOK, all_la...  64.8 us
    pallas_call x1, Pallas kernels, handover(): pl.pallas_call(handover_kernel, grid=(steps,), out_shape=[jax.ShapeDtypeS...  2.84 us

profile of v5, /device:TPU:1, one launch (start us, length us, event | category | flops | bytes accessed | tf_op | source)
XLA Modules:
  0.0 68.3 jit_solution(13152029953393960128)
XLA Ops:
  0.6 64.8 %shard_map.100 = (bf16[128,4096]{1,0:T(8,128)(2,1)}, bf16[128,4096]{1,0:T(8,128)(2,1)}, bf16[1,128,512]{2,1,0:T(8,128)(2,1)}, bf16[1,128,512]{2,1,0:T(8,128)(2,1)}, f32[8,128]{1,0:T(8,128)}, /*index=5*/f32[2,256]{1,0:T(2,128)}) custom-call(s32[64]{0:T(128)} %order_hbm.1, bf16[128,4096]{1,0:T(8,128)(2,1)} %bitcast.6, bf16[128,4096]{1,0:T(8,128)(2,1)} %bitcast.7, ...), custom_call_target="tpu_custom_call" | custom-call | tf_op jit(solution)/shard_map/pallas_call | solution.py:516
  65.4 2.8 %shard_map.101 = (bf16[128,4096]{1,0:T(8,128)(2,1)}, bf16[128,4096]{1,0:T(8,128)(2,1)}, bf16[1,128,512]{2,1,0:T(8,128)(2,1)}, bf16[1,128,512]{2,1,0:T(8,128)(2,1)}, f32[8,128]{1,0:T(8,128)}, /*index=5*/f32[2,256]{1,0:T(2,128)}) custom-call(bf16[128,4096]{1,0:T(8,128)(2,1)} %get-tuple-element.18.refs_0_, bf16[128,4096]{1,0:T(8,128)(2,1)} %get-tuple-element.19.refs_1_, ...), custom_call_target="tpu_custom_call" | custom-call | tf_op jit(solution)/shard_map/pallas_call | solution.py:565
